TPU v7x, 32 devices: a whole 2x2x4 slice. The times are simulated.
32 devices in a mesh: seq: 8 (over z, core), tensor: 4 (over y, x).
Axes of the slice: x: 2, y: 2, z: 4, core: 2. Of those that a mesh axis runs over, the one named last changes fastest.
Arguments:
- tokens: bfloat16 [2, 1024, 3072], P(None, ('seq', 'tensor')), may hold values from -6 to 6
- qkv_weight: bfloat16 [48, 192, 3072], P('tensor'), may hold values from -0.109375 to 0.109375
- rate_weight: bfloat16 [48, 3072], P('tensor'), may hold values from -0.109375 to 0.109375
- base_rate: float32 [48], P('tensor'), may hold values from 0.003 to 0.03
- first_w: float32 [48, 64, 256], P('tensor'), may hold values from -0.75 to 0.75
- first_b: float32 [48, 256], P('tensor'), may hold values from -3 to 3
- second_w: float32 [48, 256, 64], P('tensor'), may hold values from -0.375 to 0.375
- second_b: float32 [48, 64], P('tensor'), may hold values from -3 to 3
- norm_gain: float32 [48, 64], P('tensor'), may hold values from 0.5 to 1.5
- norm_shift: float32 [48, 64], P('tensor'), may hold values from -3 to 3
- out_weight: bfloat16 [3072, 3072], P('tensor'), may hold values from -0.109375 to 0.109375
Outputs:
- mixed: bfloat16 [2, 1024, 3072], P(None, ('seq', 'tensor'))
All inputs are finite; a program needn't handle non-finite values.
Results may differ from a plain program's by a relative error of at most 0.019.
Values may be sent and summed in bfloat16 or wider, within the bound.
A program may use at most 64 MiB of HBM per device.

v0:
```python
import jax
import jax.numpy as jnp
from jax import lax
from jax.sharding import PartitionSpec as P

HEAD = 64
MB = 64


def as_sent(value):

    def short(part):
        return part.astype(jnp.bfloat16) if part.dtype == jnp.float32 else part

    return jax.tree.map(short, value)


def shifted(value, axis, steps):
    count = lax.axis_size(axis)
    first, last = (max(0, -steps), min(count, count - steps))
    return lax.ppermute(value, axis, [(source, source + steps) for source in range(first, last)])


def smooth_gate(values):
    return jax.nn.gelu(values, approximate=True)


def apply_model(rows, weights, norm_gain, norm_shift):
    first_w, first_b, second_w, second_b = weights
    pre_act = (
        jnp.dot(rows, first_w.astype(jnp.bfloat16), preferred_element_type=jnp.float32) + first_b
    )
    hidden = smooth_gate(pre_act).astype(jnp.bfloat16)
    outer = (
        jnp.dot(hidden, second_w.astype(jnp.bfloat16), preferred_element_type=jnp.float32)
        + second_b
    )
    average = jnp.mean(outer, axis=-1, keepdims=True)
    centered = outer - average
    inverse = lax.rsqrt(jnp.mean(centered * centered, axis=-1, keepdims=True) + 1e-06)
    normed = centered * inverse
    return (pre_act, hidden, normed, inverse, norm_gain * normed + norm_shift)


def block_update(weights, block, norm_gain, norm_shift):
    queries, key_rows, value_rows, rates = block
    first_w, first_b, second_w, second_b = weights
    pre_act, hidden, normed, inverse, predicted = apply_model(
        key_rows, weights, norm_gain, norm_shift
    )
    target = value_rows.astype(jnp.float32) - key_rows.astype(jnp.float32)
    upstream = (predicted - target) * norm_gain
    grad_outer = inverse * (
        upstream
        - jnp.mean(upstream, axis=-1, keepdims=True)
        - normed * jnp.mean(upstream * normed, axis=-1, keepdims=True)
    )
    weighted_outer = rates[:, None] * grad_outer
    scaled_outer = weighted_outer.astype(jnp.bfloat16)
    plain_outer = grad_outer.astype(jnp.bfloat16)
    grad_hidden = jnp.dot(
        plain_outer, second_w.astype(jnp.bfloat16).T, preferred_element_type=jnp.float32
    )
    unused, pullback = jax.vjp(smooth_gate, pre_act)
    grad_inner = pullback(grad_hidden)[0]
    weighted_inner = rates[:, None] * grad_inner
    scaled_inner = weighted_inner.astype(jnp.bfloat16)
    new_weights = (
        first_w - jnp.dot(key_rows.T, scaled_inner, preferred_element_type=jnp.float32),
        first_b - jnp.sum(weighted_inner, axis=0),
        second_w - jnp.dot(hidden.T, scaled_outer, preferred_element_type=jnp.float32),
        second_b - jnp.sum(weighted_outer, axis=0),
    )
    answer = apply_model(queries, new_weights, norm_gain, norm_shift)[4] + queries.astype(
        jnp.float32
    )
    return (new_weights, answer.astype(jnp.bfloat16))


def head_chain(weights, queries, key_rows, value_rows, rates, norm_gain, norm_shift):
    block_count = queries.shape[0] // MB
    stacked = (
        queries.reshape(block_count, MB, -1),
        key_rows.reshape(block_count, MB, -1),
        value_rows.reshape(block_count, MB, -1),
        rates.reshape(block_count, MB),
    )

    def head_advance(state, block):
        return block_update(state, block, norm_gain, norm_shift)

    final, produced = lax.scan(head_advance, weights, stacked)
    return (final, produced.reshape(queries.shape[0], -1))


def shards(
    tokens,
    qkv_weight,
    rate_weight,
    base_rate,
    first_w,
    first_b,
    second_w,
    second_b,
    norm_gain,
    norm_shift,
    out_weight,
):
    group_size = lax.axis_size("tensor")
    seq_count = tokens.shape[0]
    row_count = tokens.shape[1] * group_size
    head_count = first_w.shape[0]
    qkv_local = qkv_weight.reshape(-1, qkv_weight.shape[2])
    contract = (((2,), (1,)), ((), ()))
    piece = lax.all_gather(tokens, "tensor", axis=1, tiled=True)
    block_proj = lax.dot_general(piece, qkv_local, contract, preferred_element_type=jnp.float32)
    block_logit = lax.dot_general(piece, rate_weight, contract, preferred_element_type=jnp.float32)
    projected = block_proj
    projected = projected.astype(jnp.bfloat16).reshape(seq_count, row_count, head_count, 3 * HEAD)
    queries = projected[:, :, :, :HEAD]
    key_rows = projected[:, :, :, HEAD : 2 * HEAD]
    value_rows = projected[:, :, :, 2 * HEAD :]
    rates = base_rate * jax.nn.sigmoid(block_logit)
    weights = (first_w, first_b, second_w, second_b)
    position = lax.axis_index("seq")
    chain_length = lax.axis_size("seq")
    buffer = jnp.zeros((seq_count, row_count, head_count, HEAD), jnp.bfloat16)
    head_chains = jax.vmap(head_chain, in_axes=((0, 0, 0, 0), 1, 1, 1, 1, 0, 0), out_axes=(0, 1))
    seq_chains = jax.vmap(
        head_chains, in_axes=((0, 0, 0, 0), 0, 0, 0, 0, None, None), out_axes=(0, 0)
    )
    start_state = tuple(
        (jnp.broadcast_to(member[None], (seq_count,) + member.shape) for member in weights)
    )

    def turn(section, state):
        current, outputs = state

        def turn_advance(unused):
            return seq_chains(current, queries, key_rows, value_rows, rates, norm_gain, norm_shift)

        def remain(unused):
            return (current, outputs)

        updated, outputs = lax.cond(position == section, turn_advance, remain, 0)
        passed = jax.tree.map(
            lambda part, own: part.astype(own.dtype), shifted(as_sent(updated), "seq", 1), updated
        )
        return (passed, outputs)

    unused, outputs = lax.fori_loop(0, chain_length, turn, (start_state, buffer))
    flat_out = outputs.reshape(seq_count, row_count, -1)
    partial_out = lax.dot_general(
        flat_out, out_weight, (((2,), (0,)), ((), ())), preferred_element_type=jnp.float32
    )
    return lax.psum_scatter(
        partial_out.astype(jnp.bfloat16), "tensor", scatter_dimension=1, tiled=True
    )


def solution(mesh):
    in_specs = (
        P(None, ("seq", "tensor"), None),
        P("tensor", None, None),
        P("tensor", None),
        P("tensor"),
        P("tensor", None, None),
        P("tensor", None),
        P("tensor", None, None),
        P("tensor", None),
        P("tensor", None),
        P("tensor", None),
        P("tensor", None),
    )
    out_specs = P(None, ("seq", "tensor"), None)
    return jax.shard_map(shards, mesh=mesh, in_specs=in_specs, out_specs=out_specs, check_vma=False)
```

profile of v0, /device:TPU:24, one launch (start us, length us, event | category | flops | bytes accessed | tf_op | source)
XLA Modules:
  0.0 647.5 jit_solution(13741937401383501775)
XLA Ops:
  7.3 33.9 %all-gather.2.cloned.1.call-done = bf16[2,128,3072]{2,1,0:T(8,128)(2,1)} async-done(((bf16[2,32,3072]{2,1,0:T(8,128)(2,1)}), bf16[2,128,3072]{2,1,0:T(8,128)(2,1)}) %all-gather.2.cloned.1.call-update) | async-done | bytes 1572880 | tf_op jit(solution)/shard_map/all_gather | solution.py:115
  43.3 7.2 %convolution_convert_fusion = bf16[2,128,2304]{2,1,0:T(8,128)(2,1)S(1)} fusion(bf16[2,128,3072]{2,1,0:T(8,128)(2,1)S(1)} %copy-done.7, bf16[2304,3072,1]{1,0,2:T(8,128)(2,1)} %bitcast.114), kind=kOutput, calls=%fused_computation.77 | convolution fusion | flops 3624468480 | bytes 16908288 | tf_op jit(solution)/shard_map/dot_general | solution.py:116
  54.8 548.4 %while.41 = (s32[]{:T(128)}, f32[2,12,64,256]{3,2,1,0:T(8,128)S(1)}, f32[2,12,256]{2,1,0:T(8,128)S(1)}, f32[2,12,256,64]{2,3,1,0:T(8,128)S(1)}, f32[2,12,64]{2,1...) while((s32[]{:T(128)}, ...), condition=%wide.region_13.14_spmd, body=%wide.region_0.13_spmd.sunk | while | flops 381339648 | bytes 75709272 | solution.py:151
  64.5 13.5 %collective-permute-done.3 = bf16[2,12,64]{2,1,0:T(8,128)(2,1)S(1)} collective-permute-done((bf16[2,12,64]{2,1,0:T(8,128)(2,1)S(1)}, bf16[2,12,64]{2,1,0:T(8,128)(2,1)S(1)}, u32[]{:S(2)}, u32[]{:S(2)}) %collective-permute-start.3) | collective-permute-done | bytes 3104 | tf_op jit(solution)/shard_map/while/body/eval_jaxpr/ppermute | solution.py:21
  90.4 13.5 %collective-permute-done.3 = bf16[2,12,64]{2,1,0:T(8,128)(2,1)S(1)} collective-permute-done((bf16[2,12,64]{2,1,0:T(8,128)(2,1)S(1)}, bf16[2,12,64]{2,1,0:T(8,128)(2,1)S(1)}, u32[]{:S(2)}, u32[]{:S(2)}) %collective-permute-start.3) | collective-permute-done | bytes 3104 | tf_op jit(solution)/shard_map/while/body/eval_jaxpr/ppermute | solution.py:21
  116.2 13.5 %collective-permute-done.3 = bf16[2,12,64]{2,1,0:T(8,128)(2,1)S(1)} collective-permute-done((bf16[2,12,64]{2,1,0:T(8,128)(2,1)S(1)}, bf16[2,12,64]{2,1,0:T(8,128)(2,1)S(1)}, u32[]{:S(2)}, u32[]{:S(2)}) %collective-permute-start.3) | collective-permute-done | bytes 3104 | tf_op jit(solution)/shard_map/while/body/eval_jaxpr/ppermute | solution.py:21
  142.1 13.5 %collective-permute-done.3 = bf16[2,12,64]{2,1,0:T(8,128)(2,1)S(1)} collective-permute-done((bf16[2,12,64]{2,1,0:T(8,128)(2,1)S(1)}, bf16[2,12,64]{2,1,0:T(8,128)(2,1)S(1)}, u32[]{:S(2)}, u32[]{:S(2)}) %collective-permute-start.3) | collective-permute-done | bytes 3104 | tf_op jit(solution)/shard_map/while/body/eval_jaxpr/ppermute | solution.py:21
  168.0 13.5 %collective-permute-done.3 = bf16[2,12,64]{2,1,0:T(8,128)(2,1)S(1)} collective-permute-done((bf16[2,12,64]{2,1,0:T(8,128)(2,1)S(1)}, bf16[2,12,64]{2,1,0:T(8,128)(2,1)S(1)}, u32[]{:S(2)}, u32[]{:S(2)}) %collective-permute-start.3) | collective-permute-done | bytes 3104 | tf_op jit(solution)/shard_map/while/body/eval_jaxpr/ppermute | solution.py:21
  193.9 272.3 %collective-permute-done.3 = bf16[2,12,64]{2,1,0:T(8,128)(2,1)S(1)} collective-permute-done((bf16[2,12,64]{2,1,0:T(8,128)(2,1)S(1)}, bf16[2,12,64]{2,1,0:T(8,128)(2,1)S(1)}, u32[]{:S(2)}, u32[]{:S(2)}) %collective-permute-start.3) | collective-permute-done | bytes 3104 | tf_op jit(solution)/shard_map/while/body/eval_jaxpr/ppermute | solution.py:21
  468.9 50.2 %conditional.2 = ((f32[2,12,64,256]{3,2,1,0:T(8,128)S(1)}, f32[2,12,256]{2,1,0:T(8,128)S(1)}, f32[2,12,256,64]{2,3,1,0:T(8,128)S(1)}, f32[2,12,64]{2,1,0:T(8,128)S(1)}, bf16[2,128,12,64]{3,1,2,0:T(8,128)(2,1)})) conditional(s32[]{:T(128)} %convert_element_type.237, (f32[2,12,64,256]{3,2,1,0:T(8,128)S(1)}, f32[2,12,256]{2,1,0:T(8,128)S(1)}, ...), branch_computations={%region_1.0_spmd, %region_2.12_spmd} | conditional | flops 379751424 | bytes 59826608 | solution.py:145
  469.0 3.1 reshape.69
  472.1 2.3 copy.22
  482.3 34.6 %while.40 = (s32[]{:T(128)}, f32[2,12,64,256]{3,2,1,0:T(8,128)S(1)}, f32[2,12,256]{2,1,0:T(8,128)S(1)}, f32[2,12,256,64]{2,3,1,0:T(8,128)}, f32[2,12,64]{2,1,0:T...) while((s32[]{:T(128)}, ...), condition=%wide.region_12.11_spmd, body=%wide.region_3.10_spmd.sunk | while | flops 379751424 | bytes 41713880 | solution.py:92
  487.0 2.7 multiply_reduce_fusion.8
  494.3 2.5 fusion.98
  497.4 2.2 fusion.99
  504.3 2.7 multiply_reduce_fusion.8
  511.6 2.5 fusion.98
  514.7 2.2 fusion.99
  528.8 13.5 %collective-permute-done.3 = bf16[2,12,64]{2,1,0:T(8,128)(2,1)S(1)} collective-permute-done((bf16[2,12,64]{2,1,0:T(8,128)(2,1)S(1)}, bf16[2,12,64]{2,1,0:T(8,128)(2,1)S(1)}, u32[]{:S(2)}, u32[]{:S(2)}) %collective-permute-start.3) | collective-permute-done | bytes 3104 | tf_op jit(solution)/shard_map/while/body/eval_jaxpr/ppermute | solution.py:21
  546.0 39.8 %collective-permute-start.2 = (bf16[2,12,256,64]{2,3,1,0:T(8,128)(2,1)}, bf16[2,12,256,64]{2,3,1,0:T(8,128)(2,1)}, u32[]{:S(2)}, u32[]{:S(2)}) collective-permute-start(bf16[2,12,256,64]{2,3,1,0:T(8,128)(2,1)} %convert_element_type.242), channel_id=1, source_target_pairs={{0,4},{4,8},{8,12},{12,16},{16,20},{20,24},{24,28},{1,5},{5,9},{9,... | collective-permute-start | bytes 2359304 | tf_op jit(solution)/shard_map/while/body/eval_jaxpr/ppermute | solution.py:21
  592.6 8.0 %collective-permute-done.3 = bf16[2,12,64]{2,1,0:T(8,128)(2,1)S(1)} collective-permute-done((bf16[2,12,64]{2,1,0:T(8,128)(2,1)S(1)}, bf16[2,12,64]{2,1,0:T(8,128)(2,1)S(1)}, u32[]{:S(2)}, u32[]{:S(2)}) %collective-permute-start.3) | collective-permute-done | bytes 3104 | tf_op jit(solution)/shard_map/while/body/eval_jaxpr/ppermute | solution.py:21
  604.6 4.9 fusion.57
  609.6 31.1 %reduce-scatter.2.cloned.1.call-done = bf16[2,32,3072]{2,1,0:T(8,128)(2,1)} async-done(((bf16[2,128,3072]{2,1,0:T(8,128)(2,1)}), bf16[2,32,3072]{2,1,0:T(8,128)(2,1)}) %reduce-scatter.2.cloned.1.call-update) | async-done | bytes 393232 | tf_op jit(solution)/shard_map/reduce_scatter | solution.py:156
  (209 shorter events, 134.3 us)
Async XLA Ops:
  6.5 34.7 %all-gather.2.cloned.1.call-start = ((), (), s32[]{:S(2)}) async-start(), calls=%async_computation.1 | async-start | bytes 1966080 | tf_op jit(solution)/shard_map/all_gather | solution.py:115
  7.3 633.4 %reduce-scatter.2.cloned.1.call-start = ((), (), s32[]{:S(2)}) async-start(), calls=%async_computation.2 | async-start | bytes 1966080 | tf_op jit(solution)/shard_map/reduce_scatter | solution.py:156
  55.8 22.2 %collective-permute-start.2 = (bf16[2,12,256,64]{2,3,1,0:T(8,128)(2,1)}, bf16[2,12,256,64]{2,3,1,0:T(8,128)(2,1)}, u32[]{:S(2)}, u32[]{:S(2)}) collective-permute-start(bf16[2,12,256,64]{2,3,1,0:T(8,128)(2,1)} %convert_element_type.242), channel_id=1, source_target_pairs={{0,4},{4,8},{8,12},{12,16},{16,20},{20,24},{24,28},{1,5},{5,9},{9,... | collective-permute-start | bytes 2359304 | tf_op jit(solution)/shard_map/while/body/eval_jaxpr/ppermute | solution.py:21
  58.7 20.6 %collective-permute-start = (bf16[2,12,64,256]{3,2,1,0:T(8,128)(2,1)}, bf16[2,12,64,256]{3,2,1,0:T(8,128)(2,1)}, u32[]{:S(2)}, u32[]{:S(2)}) collective-permute-start(bf16[2,12,64,256]{3,2,1,0:T(8,128)(2,1)} %convert_element_type.238), channel_id=1, source_target_pairs={{0,4},{4,8},{8,12},{12,16},{16,20},{20,24},{24,28},{1,5},{5,9},{9,... | collective-permute-start | bytes 2359304 | tf_op jit(solution)/shard_map/while/body/eval_jaxpr/ppermute | solution.py:21
  60.6 17.4 %collective-permute-start.1 = (bf16[2,12,256]{2,1,0:T(8,128)(2,1)S(1)}, bf16[2,12,256]{2,1,0:T(8,128)(2,1)S(1)}, u32[]{:S(2)}, u32[]{:S(2)}) collective-permute-start(bf16[2,12,256]{2,1,0:T(8,128)(2,1)S(1)} %convert_element_type.240), channel_id=1, source_target_pairs={{0,4},{4,8},{8,12},{12,16},{16,20},{20,24},{24,28},{1,5},{5,9},{9,... | collective-permute-start | bytes 36872 | tf_op jit(solution)/shard_map/while/body/eval_jaxpr/ppermute | solution.py:21
  81.6 22.2 %collective-permute-start.2 = (bf16[2,12,256,64]{2,3,1,0:T(8,128)(2,1)}, bf16[2,12,256,64]{2,3,1,0:T(8,128)(2,1)}, u32[]{:S(2)}, u32[]{:S(2)}) collective-permute-start(bf16[2,12,256,64]{2,3,1,0:T(8,128)(2,1)} %convert_element_type.242), channel_id=1, source_target_pairs={{0,4},{4,8},{8,12},{12,16},{16,20},{20,24},{24,28},{1,5},{5,9},{9,... | collective-permute-start | bytes 2359304 | tf_op jit(solution)/shard_map/while/body/eval_jaxpr/ppermute | solution.py:21
  84.6 20.6 %collective-permute-start = (bf16[2,12,64,256]{3,2,1,0:T(8,128)(2,1)}, bf16[2,12,64,256]{3,2,1,0:T(8,128)(2,1)}, u32[]{:S(2)}, u32[]{:S(2)}) collective-permute-start(bf16[2,12,64,256]{3,2,1,0:T(8,128)(2,1)} %convert_element_type.238), channel_id=1, source_target_pairs={{0,4},{4,8},{8,12},{12,16},{16,20},{20,24},{24,28},{1,5},{5,9},{9,... | collective-permute-start | bytes 2359304 | tf_op jit(solution)/shard_map/while/body/eval_jaxpr/ppermute | solution.py:21
  86.5 17.4 %collective-permute-start.1 = (bf16[2,12,256]{2,1,0:T(8,128)(2,1)S(1)}, bf16[2,12,256]{2,1,0:T(8,128)(2,1)S(1)}, u32[]{:S(2)}, u32[]{:S(2)}) collective-permute-start(bf16[2,12,256]{2,1,0:T(8,128)(2,1)S(1)} %convert_element_type.240), channel_id=1, source_target_pairs={{0,4},{4,8},{8,12},{12,16},{16,20},{20,24},{24,28},{1,5},{5,9},{9,... | collective-permute-start | bytes 36872 | tf_op jit(solution)/shard_map/while/body/eval_jaxpr/ppermute | solution.py:21
  107.5 22.2 %collective-permute-start.2 = (bf16[2,12,256,64]{2,3,1,0:T(8,128)(2,1)}, bf16[2,12,256,64]{2,3,1,0:T(8,128)(2,1)}, u32[]{:S(2)}, u32[]{:S(2)}) collective-permute-start(bf16[2,12,256,64]{2,3,1,0:T(8,128)(2,1)} %convert_element_type.242), channel_id=1, source_target_pairs={{0,4},{4,8},{8,12},{12,16},{16,20},{20,24},{24,28},{1,5},{5,9},{9,... | collective-permute-start | bytes 2359304 | tf_op jit(solution)/shard_map/while/body/eval_jaxpr/ppermute | solution.py:21
  110.4 20.6 %collective-permute-start = (bf16[2,12,64,256]{3,2,1,0:T(8,128)(2,1)}, bf16[2,12,64,256]{3,2,1,0:T(8,128)(2,1)}, u32[]{:S(2)}, u32[]{:S(2)}) collective-permute-start(bf16[2,12,64,256]{3,2,1,0:T(8,128)(2,1)} %convert_element_type.238), channel_id=1, source_target_pairs={{0,4},{4,8},{8,12},{12,16},{16,20},{20,24},{24,28},{1,5},{5,9},{9,... | collective-permute-start | bytes 2359304 | tf_op jit(solution)/shard_map/while/body/eval_jaxpr/ppermute | solution.py:21
  112.4 17.4 %collective-permute-start.1 = (bf16[2,12,256]{2,1,0:T(8,128)(2,1)S(1)}, bf16[2,12,256]{2,1,0:T(8,128)(2,1)S(1)}, u32[]{:S(2)}, u32[]{:S(2)}) collective-permute-start(bf16[2,12,256]{2,1,0:T(8,128)(2,1)S(1)} %convert_element_type.240), channel_id=1, source_target_pairs={{0,4},{4,8},{8,12},{12,16},{16,20},{20,24},{24,28},{1,5},{5,9},{9,... | collective-permute-start | bytes 36872 | tf_op jit(solution)/shard_map/while/body/eval_jaxpr/ppermute | solution.py:21
  133.4 22.2 %collective-permute-start.2 = (bf16[2,12,256,64]{2,3,1,0:T(8,128)(2,1)}, bf16[2,12,256,64]{2,3,1,0:T(8,128)(2,1)}, u32[]{:S(2)}, u32[]{:S(2)}) collective-permute-start(bf16[2,12,256,64]{2,3,1,0:T(8,128)(2,1)} %convert_element_type.242), channel_id=1, source_target_pairs={{0,4},{4,8},{8,12},{12,16},{16,20},{20,24},{24,28},{1,5},{5,9},{9,... | collective-permute-start | bytes 2359304 | tf_op jit(solution)/shard_map/while/body/eval_jaxpr/ppermute | solution.py:21
  136.3 20.6 %collective-permute-start = (bf16[2,12,64,256]{3,2,1,0:T(8,128)(2,1)}, bf16[2,12,64,256]{3,2,1,0:T(8,128)(2,1)}, u32[]{:S(2)}, u32[]{:S(2)}) collective-permute-start(bf16[2,12,64,256]{3,2,1,0:T(8,128)(2,1)} %convert_element_type.238), channel_id=1, source_target_pairs={{0,4},{4,8},{8,12},{12,16},{16,20},{20,24},{24,28},{1,5},{5,9},{9,... | collective-permute-start | bytes 2359304 | tf_op jit(solution)/shard_map/while/body/eval_jaxpr/ppermute | solution.py:21
  138.3 17.4 %collective-permute-start.1 = (bf16[2,12,256]{2,1,0:T(8,128)(2,1)S(1)}, bf16[2,12,256]{2,1,0:T(8,128)(2,1)S(1)}, u32[]{:S(2)}, u32[]{:S(2)}) collective-permute-start(bf16[2,12,256]{2,1,0:T(8,128)(2,1)S(1)} %convert_element_type.240), channel_id=1, source_target_pairs={{0,4},{4,8},{8,12},{12,16},{16,20},{20,24},{24,28},{1,5},{5,9},{9,... | collective-permute-start | bytes 36872 | tf_op jit(solution)/shard_map/while/body/eval_jaxpr/ppermute | solution.py:21
  159.3 22.2 %collective-permute-start.2 = (bf16[2,12,256,64]{2,3,1,0:T(8,128)(2,1)}, bf16[2,12,256,64]{2,3,1,0:T(8,128)(2,1)}, u32[]{:S(2)}, u32[]{:S(2)}) collective-permute-start(bf16[2,12,256,64]{2,3,1,0:T(8,128)(2,1)} %convert_element_type.242), channel_id=1, source_target_pairs={{0,4},{4,8},{8,12},{12,16},{16,20},{20,24},{24,28},{1,5},{5,9},{9,... | collective-permute-start | bytes 2359304 | tf_op jit(solution)/shard_map/while/body/eval_jaxpr/ppermute | solution.py:21
  162.2 20.6 %collective-permute-start = (bf16[2,12,64,256]{3,2,1,0:T(8,128)(2,1)}, bf16[2,12,64,256]{3,2,1,0:T(8,128)(2,1)}, u32[]{:S(2)}, u32[]{:S(2)}) collective-permute-start(bf16[2,12,64,256]{3,2,1,0:T(8,128)(2,1)} %convert_element_type.238), channel_id=1, source_target_pairs={{0,4},{4,8},{8,12},{12,16},{16,20},{20,24},{24,28},{1,5},{5,9},{9,... | collective-permute-start | bytes 2359304 | tf_op jit(solution)/shard_map/while/body/eval_jaxpr/ppermute | solution.py:21
  164.1 17.4 %collective-permute-start.1 = (bf16[2,12,256]{2,1,0:T(8,128)(2,1)S(1)}, bf16[2,12,256]{2,1,0:T(8,128)(2,1)S(1)}, u32[]{:S(2)}, u32[]{:S(2)}) collective-permute-start(bf16[2,12,256]{2,1,0:T(8,128)(2,1)S(1)} %convert_element_type.240), channel_id=1, source_target_pairs={{0,4},{4,8},{8,12},{12,16},{16,20},{20,24},{24,28},{1,5},{5,9},{9,... | collective-permute-start | bytes 36872 | tf_op jit(solution)/shard_map/while/body/eval_jaxpr/ppermute | solution.py:21
  185.2 281.0 %collective-permute-start.2 = (bf16[2,12,256,64]{2,3,1,0:T(8,128)(2,1)}, bf16[2,12,256,64]{2,3,1,0:T(8,128)(2,1)}, u32[]{:S(2)}, u32[]{:S(2)}) collective-permute-start(bf16[2,12,256,64]{2,3,1,0:T(8,128)(2,1)} %convert_element_type.242), channel_id=1, source_target_pairs={{0,4},{4,8},{8,12},{12,16},{16,20},{20,24},{24,28},{1,5},{5,9},{9,... | collective-permute-start | bytes 2359304 | tf_op jit(solution)/shard_map/while/body/eval_jaxpr/ppermute | solution.py:21
  188.1 279.4 %collective-permute-start = (bf16[2,12,64,256]{3,2,1,0:T(8,128)(2,1)}, bf16[2,12,64,256]{3,2,1,0:T(8,128)(2,1)}, u32[]{:S(2)}, u32[]{:S(2)}) collective-permute-start(bf16[2,12,64,256]{3,2,1,0:T(8,128)(2,1)} %convert_element_type.238), channel_id=1, source_target_pairs={{0,4},{4,8},{8,12},{12,16},{16,20},{20,24},{24,28},{1,5},{5,9},{9,... | collective-permute-start | bytes 2359304 | tf_op jit(solution)/shard_map/while/body/eval_jaxpr/ppermute | solution.py:21
  190.0 276.2 %collective-permute-start.1 = (bf16[2,12,256]{2,1,0:T(8,128)(2,1)S(1)}, bf16[2,12,256]{2,1,0:T(8,128)(2,1)S(1)}, u32[]{:S(2)}, u32[]{:S(2)}) collective-permute-start(bf16[2,12,256]{2,1,0:T(8,128)(2,1)S(1)} %convert_element_type.240), channel_id=1, source_target_pairs={{0,4},{4,8},{8,12},{12,16},{16,20},{20,24},{24,28},{1,5},{5,9},{9,... | collective-permute-start | bytes 36872 | tf_op jit(solution)/shard_map/while/body/eval_jaxpr/ppermute | solution.py:21
  192.0 274.2 %collective-permute-start.3 = (bf16[2,12,64]{2,1,0:T(8,128)(2,1)S(1)}, bf16[2,12,64]{2,1,0:T(8,128)(2,1)S(1)}, u32[]{:S(2)}, u32[]{:S(2)}) collective-permute-start(bf16[2,12,64]{2,1,0:T(8,128)(2,1)S(1)} %convert_element_type.244), channel_id=1, source_target_pairs={{0,4},{4,8},{8,12},{12,16},{16,20},{20,24},{24,28},{1,5},{5,9},{9,... | collective-permute-start | bytes 9224 | tf_op jit(solution)/shard_map/while/body/eval_jaxpr/ppermute | solution.py:21
  520.1 22.2 %collective-permute-start.2 = (bf16[2,12,256,64]{2,3,1,0:T(8,128)(2,1)}, bf16[2,12,256,64]{2,3,1,0:T(8,128)(2,1)}, u32[]{:S(2)}, u32[]{:S(2)}) collective-permute-start(bf16[2,12,256,64]{2,3,1,0:T(8,128)(2,1)} %convert_element_type.242), channel_id=1, source_target_pairs={{0,4},{4,8},{8,12},{12,16},{16,20},{20,24},{24,28},{1,5},{5,9},{9,... | collective-permute-start | bytes 2359304 | tf_op jit(solution)/shard_map/while/body/eval_jaxpr/ppermute | solution.py:21
  523.0 20.6 %collective-permute-start = (bf16[2,12,64,256]{3,2,1,0:T(8,128)(2,1)}, bf16[2,12,64,256]{3,2,1,0:T(8,128)(2,1)}, u32[]{:S(2)}, u32[]{:S(2)}) collective-permute-start(bf16[2,12,64,256]{3,2,1,0:T(8,128)(2,1)} %convert_element_type.238), channel_id=1, source_target_pairs={{0,4},{4,8},{8,12},{12,16},{16,20},{20,24},{24,28},{1,5},{5,9},{9,... | collective-permute-start | bytes 2359304 | tf_op jit(solution)/shard_map/while/body/eval_jaxpr/ppermute | solution.py:21
  546.0 54.6 %collective-permute-start.2 = (bf16[2,12,256,64]{2,3,1,0:T(8,128)(2,1)}, bf16[2,12,256,64]{2,3,1,0:T(8,128)(2,1)}, u32[]{:S(2)}, u32[]{:S(2)}) collective-permute-start(bf16[2,12,256,64]{2,3,1,0:T(8,128)(2,1)} %convert_element_type.242), channel_id=1, source_target_pairs={{0,4},{4,8},{8,12},{12,16},{16,20},{20,24},{24,28},{1,5},{5,9},{9,... | collective-permute-start | bytes 2359304 | tf_op jit(solution)/shard_map/while/body/eval_jaxpr/ppermute | solution.py:21
  (24 other events, 201.4 us)
Sparse Core Ops, SparseCore 0:
  9.2 31.9 all-gather.1
  609.7 30.9 reduce-scatter.1
where the time goes:
time: 651 us; the launch traced here: 648 us
  waiting for transfers between devices  427 us (66%)
  starting transfers between devices  99.2 us (15%)
  other arithmetic  52.8 us (8%)
  matrix products  28.1 us (4%)
  local copies, waits for them, and re-layouts  25.6 us (4%)
  between operations  13.5 us (2%)
    ppermute x32, waiting for transfers between devices, shifted(): lax.ppermute(value, axis, [(source, source + steps) for source in range(f...  361 us
    ppermute x32, starting transfers between devices, shifted(): lax.ppermute(value, axis, [(source, source + steps) for source in range(f...  99.1 us
    all_gather x1, waiting for transfers between devices, shards(): piece = lax.all_gather(tokens, 'tensor', axis=1, tiled=True)  33.9 us
    reduce_scatter x1, waiting for transfers between devices, shards(): lax.psum_scatter(partial_out.astype(jnp.bfloat16), 'tensor', scatter_dime...  31.1 us
    convert_element_type x32, other arithmetic, turn(): part.astype(own.dtype)  20.9 us
    convert_element_type x32, other arithmetic, short(): return part.astype(jnp.bfloat16) if part.dtype == jnp.float32 else part  15.9 us
  transfers between devices with their start and end apart: 34, of which 10 were waited for; matrix products, arithmetic and copies ran while one was open for 3% of the time, Pallas kernels for 0%

commit v1 on v0

v1 whole, which is shorter than its diff:
```python
import functools
import math

import jax
import jax.numpy as jnp
from jax import lax
from jax.experimental import pallas as pl
from jax.experimental.pallas import tpu as pltpu
from jax.sharding import PartitionSpec as P

HEAD = 64
MB = 64
TILE = 128
ROWS = 3 * HEAD + 16
CURVE = math.sqrt(2.0 / math.pi)
CUBIC = 0.044715
F32 = jnp.float32
BF16 = jnp.bfloat16
NN = (((1,), (0,)), ((), ()))
NT = (((1,), (1,)), ((), ()))


def dot(a, b, dims=NN):
    return lax.dot_general(a, b, dims, preferred_element_type=F32)


def split_bias(state):
    lane = lax.broadcasted_iota(jnp.int32, state.shape, 1)
    rest = state - state.astype(BF16).astype(F32)
    return jnp.where(lane == HEAD + 1, rest, state).astype(BF16)


def mean_rows(values):
    return jnp.sum(values, axis=0, keepdims=True) * (1.0 / HEAD)


def load_state(count, first, second, second_t, state):
    w1, w2, w2t, w1b, w2b, w2tb = state
    for c in range(count):
        w1[c] = first[c]
        w2[c] = second[c]
        w2t[c] = second_t[c]
        w1b[c] = split_bias(first[c])
        w2b[c] = second[c].astype(BF16)
        w2tb[c] = second_t[c].astype(BF16)


def mini_batch(count, keys_low, learn, key_tile, query_tile, consts, state, bias2):
    gain, shift = consts
    w1, w2, w2t, w1b, w2b, w2tb = state
    each = range(count)
    lane = lax.broadcasted_iota(jnp.int32, (HEAD, TILE), 1)
    is_key = (lane < MB) if keys_low else (lane >= MB)
    row = lax.broadcasted_iota(jnp.int32, (HEAD, TILE), 0)
    ones_rows = jnp.where(row < 2, 1.0, 0.0)
    rows = [
        jnp.where(
            is_key,
            key_tile[c, HEAD : 2 * HEAD, :].astype(F32),
            query_tile[c, :HEAD, :].astype(F32),
        )
        for c in each
    ]
    wide = [jnp.concatenate([rows[c], ones_rows], axis=0).astype(BF16) for c in each]
    pre = [dot(w1b[c], wide[c]) for c in each]
    square = [p * p for p in pre]
    bend = [jnp.tanh((CURVE * p) * (1.0 + CUBIC * s)) for p, s in zip(pre, square)]
    half = [0.5 + 0.5 * t for t in bend]
    hidden = [(p * h).astype(BF16) for p, h in zip(pre, half)]
    outer = [dot(w2tb[c], hidden[c]) + bias2[c] for c in each]
    centered = [o - mean_rows(o) for o in outer]
    inverse = [lax.rsqrt(mean_rows(z * z) + 1e-06) for z in centered]
    normed = [z * i for z, i in zip(centered, inverse)]
    model = [gain[c] * normed[c] + shift[c] for c in each]
    answer = [rows[c] + model[c] for c in each]
    if not learn:
        return answer
    values = [key_tile[c, 2 * HEAD : 3 * HEAD, :].astype(F32) for c in each]
    upstream = [(model[c] - (values[c] - rows[c])) * gain[c] for c in each]
    grad_outer = [
        inverse[c]
        * (
            upstream[c]
            - mean_rows(upstream[c])
            - normed[c] * mean_rows(upstream[c] * normed[c])
        )
        for c in each
    ]
    rates = []
    for c in each:
        pair = key_tile[c, 3 * HEAD : 3 * HEAD + 16, :].astype(F32)
        rate = pair[0:1, :] + pair[1:2, :]
        rates.append(jnp.where(is_key[0:1, :], rate, 0.0))
    plain = [g.astype(BF16) for g in grad_outer]
    scaled_outer = [(rates[c] * grad_outer[c]).astype(BF16) for c in each]
    grad_hidden = [dot(w2b[c], plain[c]) for c in each]
    slope = [
        half[c]
        + (0.5 * CURVE) * pre[c] * (1.0 - bend[c] * bend[c]) * (1.0 + (3.0 * CUBIC) * square[c])
        for c in each
    ]
    scaled_inner = [(grad_hidden[c] * slope[c] * rates[c]).astype(BF16) for c in each]
    ones = jnp.ones((TILE, TILE), BF16)
    for c in each:
        new = w1[c] - dot(scaled_inner[c], wide[c], NT)
        w1[c] = new
        w1b[c] = split_bias(new)
    for c in each:
        new = w2t[c] - dot(scaled_outer[c], hidden[c], NT)
        w2t[c] = new
        w2tb[c] = new.astype(BF16)
        bias2[c] = bias2[c] - dot(scaled_outer[c], ones, NT)
        new = w2[c] - dot(hidden[c], scaled_outer[c], NT)
        w2[c] = new
        w2b[c] = new.astype(BF16)
    return answer


def chain_kernel(tiles, count, x, first, second, second_t, bias, gain, shift, out,
                 w1, w2, w2t, w1b, w2b, w2tb, bias2, low):
    state = (w1, w2, w2t, w1b, w2b, w2tb)
    load_state(count, first, second, second_t, state)
    bias2[...] = bias[...]
    low[...] = jnp.zeros_like(low)
    consts = (gain, shift)
    lane = lax.broadcasted_iota(jnp.int32, (HEAD, TILE), 1)

    def finish(tile, answer):
        for c in range(count):
            out[tile, c] = jnp.where(lane < MB, low[c], answer[c]).astype(BF16)

    def body(tile, carry):
        before = jnp.maximum(tile - 1, 0)
        answer = mini_batch(
            count, True, True, x.at[tile], x.at[before], consts, state, bias2
        )
        finish(before, answer)
        answer = mini_batch(
            count, False, True, x.at[tile], x.at[tile], consts, state, bias2
        )
        for c in range(count):
            low[c] = answer[c]
        return carry

    lax.fori_loop(0, tiles, body, 0)
    answer = mini_batch(
        count, True, False, x.at[tiles - 1], x.at[tiles - 1], consts, state, bias2
    )
    finish(tiles - 1, answer)


def run_chains(x, first, second, second_t, bias, gain, shift):
    tiles, count = x.shape[:2]
    inner = second.shape[1]
    vmem = pl.BlockSpec(memory_space=pltpu.VMEM)
    return pl.pallas_call(
        functools.partial(chain_kernel, tiles, count),
        out_shape=jax.ShapeDtypeStruct((tiles, count, HEAD, TILE), BF16),
        in_specs=[vmem] * 7,
        out_specs=vmem,
        scratch_shapes=[
            pltpu.VMEM((count, inner, TILE), F32),
            pltpu.VMEM((count, inner, HEAD), F32),
            pltpu.VMEM((count, HEAD, inner), F32),
            pltpu.VMEM((count, inner, TILE), BF16),
            pltpu.VMEM((count, inner, HEAD), BF16),
            pltpu.VMEM((count, HEAD, inner), BF16),
            pltpu.VMEM((count, HEAD, TILE), F32),
            pltpu.VMEM((count, HEAD, TILE), F32),
        ],
        compiler_params=pltpu.CompilerParams(vmem_limit_bytes=32 * 1024 * 1024),
    )(x, first, second, second_t, bias, gain, shift)


def chain_params(heads, count, first_w, first_b, second_w, second_b, norm_gain, norm_shift, total):
    ids = jnp.minimum(lax.axis_index("seq") * count + jnp.arange(count), total - 1) % heads
    inner = first_w.shape[2]

    def pick(member):
        return jnp.take(member, ids, axis=0)

    def column(member):
        return jnp.broadcast_to(pick(member)[:, :, None], (count, HEAD, TILE))

    bias_lanes = jnp.broadcast_to(pick(first_b)[:, :, None], (count, inner, 2))
    first = jnp.concatenate(
        [
            jnp.swapaxes(pick(first_w), 1, 2),
            bias_lanes,
            jnp.zeros((count, inner, TILE - HEAD - 2), F32),
        ],
        axis=2,
    )
    second = pick(second_w)
    return (
        first, second, jnp.swapaxes(second, 1, 2),
        column(second_b), column(norm_gain), column(norm_shift),
    )


def shards(
    tokens,
    qkv_weight,
    rate_weight,
    base_rate,
    first_w,
    first_b,
    second_w,
    second_b,
    norm_gain,
    norm_shift,
    out_weight,
):
    places = lax.axis_size("seq")
    seqs, _, width = tokens.shape
    block = tokens.shape[1] * lax.axis_size("tensor")
    heads = first_w.shape[0]
    assert block % TILE == 0
    parts = block // TILE
    total = seqs * heads
    count = -(-total // places)
    params = chain_params(
        heads, count, first_w, first_b, second_w, second_b, norm_gain, norm_shift, total
    )
    piece = lax.all_gather(tokens, "tensor", axis=1, tiled=True)
    contract = (((1,), (2,)), ((), ()))
    projected = lax.dot_general(
        qkv_weight.reshape(-1, width), piece, contract, preferred_element_type=F32
    ).astype(BF16)
    projected = projected.reshape(heads, 3 * HEAD, seqs, block).transpose(2, 0, 1, 3)
    logit = lax.dot_general(rate_weight, piece, contract, preferred_element_type=F32)
    rates = (base_rate[:, None, None] * jax.nn.sigmoid(logit)).transpose(1, 0, 2)[:, :, None, :]
    coarse = lax.reduce_precision(rates, 8, 7)
    load = jnp.concatenate(
        [
            projected,
            coarse.astype(BF16),
            (rates - coarse).astype(BF16),
            jnp.zeros((seqs, heads, 14, block), BF16),
        ],
        axis=2,
    ).reshape(total, ROWS, block)
    load = jnp.pad(load, ((0, places * count - total), (0, 0), (0, 0)))
    load = load.reshape(places, count, ROWS, block)
    arrived = lax.all_to_all(load, "seq", 0, 0)
    arrived = arrived.reshape(places, count, ROWS, parts, TILE).transpose(0, 3, 1, 2, 4)
    answers = run_chains(arrived.reshape(places * parts, count, ROWS, TILE), *params)
    answers = answers.reshape(places, parts, count, HEAD, TILE).transpose(0, 2, 3, 1, 4)
    answers = lax.all_to_all(answers.reshape(places, count, HEAD, block), "seq", 0, 0)
    answers = answers.reshape(places * count, HEAD, block)[:total]
    answers = answers.reshape(seqs, heads * HEAD, block)
    partial = lax.dot_general(
        answers, out_weight, (((1,), (0,)), ((), ())), preferred_element_type=F32
    ).astype(BF16)
    return lax.psum_scatter(partial, "tensor", scatter_dimension=1, tiled=True)


def solution(mesh):
    in_specs = (
        P(None, ("seq", "tensor"), None),
        P("tensor", None, None),
        P("tensor", None),
        P("tensor"),
        P("tensor", None, None),
        P("tensor", None),
        P("tensor", None, None),
        P("tensor", None),
        P("tensor", None),
        P("tensor", None),
        P("tensor", None),
    )
    out_specs = P(None, ("seq", "tensor"), None)
    return jax.shard_map(shards, mesh=mesh, in_specs=in_specs, out_specs=out_specs, check_vma=False)
```

time: 651 us -> 160 us (0.25)
  waiting for transfers between devices: 427 us -> 88.7 us
  starting transfers between devices: 99.2 us -> 5.27 us
  other arithmetic: 52.8 us -> 2.08 us
  local copies, waits for them, and re-layouts: 25.6 us -> 5.44 us
  blocking collectives: 0 us -> 14.9 us
  Pallas kernels: 0 us -> 14.2 us
  matrix products: 28.1 us -> 14.1 us
    ppermute x32 -> x0, waiting for transfers between devices: 361 us -> none  [shifted(): lax.ppermute(value, axis, [(source, source + steps) for source in range(f...]
    ppermute x32 -> x0, starting transfers between devices: 99.1 us -> none  [shifted(): lax.ppermute(value, axis, [(source, source + steps) for source in range(f...]
    convert_element_type x64 -> x0, other arithmetic: 36.8 us -> none  [the longest x32 20.9 us: turn(): part.astype(own.dtype)]
    all_to_all x0 -> x1, waiting for transfers between devices: none -> 23.1 us  [shards(): arrived = lax.all_to_all(load, 'seq', 0, 0)]
    all_to_all x0 -> x1, blocking collectives: none -> 14.9 us  [shards(): lax.all_to_all(answers.reshape(places, count, HEAD, block), 'seq', 0, 0)]
    pallas_call x0 -> x1, Pallas kernels: none -> 14.2 us  [run_chains(): pl.pallas_call(functools.partial(chain_kernel, tiles, count), out_shape=j...]
    dot_general x15 -> x3, matrix products: 28.1 us -> 14.1 us  [the longest x1 7.14 us: shards(): lax.dot_general(qkv_weight.reshape(-1, width), piece, contract, preferred...]
    while x13 -> x0, local copies, waits for them, and re-layouts: 11.7 us -> none  [the longest x3 5.91 us: head_chain(): final, produced = lax.scan(head_advance, weights, stacked)]
  transfers between devices with their start and end apart: 34 -> 3, of which waited for: 10 -> 3; matrix products, arithmetic and copies ran while one was open for 3% -> 4% of each run, Pallas kernels for 0% -> 0%
where the time goes in v1:
time: 160 us; the launch traced here: 158 us
  waiting for transfers between devices  88.7 us (55%)
  blocking collectives  14.9 us (9%)
  Pallas kernels  14.2 us (9%)
  matrix products  14.1 us (9%)
  between operations  13.6 us (8%)
  local copies, waits for them, and re-layouts  5.44 us (3%)
  starting transfers between devices  5.27 us (3%)
  other arithmetic  2.08 us (1%)
    all_gather x1, waiting for transfers between devices, shards(): piece = lax.all_gather(tokens, 'tensor', axis=1, tiled=True)  33.8 us
    reduce_scatter x1, waiting for transfers between devices, shards(): return lax.psum_scatter(partial, 'tensor', scatter_dimension=1, tiled=True)  31.1 us
    all_to_all x1, waiting for transfers between devices, shards(): arrived = lax.all_to_all(load, 'seq', 0, 0)  23.1 us
    all_to_all x1, blocking collectives, shards(): lax.all_to_all(answers.reshape(places, count, HEAD, block), 'seq', 0, 0)  14.9 us
    pallas_call x1, Pallas kernels, run_chains(): pl.pallas_call(functools.partial(chain_kernel, tiles, count), out_shape=j...  14.2 us
    dot_general x1, matrix products, shards(): lax.dot_general(qkv_weight.reshape(-1, width), piece, contract, preferred...  7.14 us
    all_to_all x1, starting transfers between devices, shards(): arrived = lax.all_to_all(load, 'seq', 0, 0)  5.23 us
    dot_general x1, matrix products, shards(): lax.dot_general(answers, out_weight, (((1,), (0,)), ((), ())), preferred_...  4.92 us
  transfers between devices with their start and end apart: 3, of which 3 were waited for; matrix products, arithmetic and copies ran while one was open for 4% of the time, Pallas kernels for 0%

profile of v1, /device:TPU:24, one launch (start us, length us, event | category | flops | bytes accessed | tf_op | source)
XLA Modules:
  0.0 158.4 jit_solution(5404264301244952216)
XLA Ops:
  6.5 0.7 all-gather.2.cloned.1.call-update
  7.3 33.8 %all-gather.2.cloned.1.call-done = bf16[2,128,3072]{2,1,0:T(8,128)(2,1)} async-done(((bf16[2,32,3072]{2,1,0:T(8,128)(2,1)}), bf16[2,128,3072]{2,1,0:T(8,128)(2,1)}) %all-gather.2.cloned.1.call-update) | async-done | bytes 1572880 | tf_op jit(solution)/shard_map/all_gather | solution.py:225
  41.2 2.1 %reduce-precision_convert_fusion = (bf16[2,12,128]{2,1,0:T(8,128)(2,1)S(1)}, bf16[2,12,128]{2,1,0:T(8,128)(2,1)S(1)}) fusion(bf16[2,128,3072]{2,1,0:T(8,128)(2,1)} %all-gather.2.cloned.1.call-done, bf16[12,3072]{1,0:T(8,128)(2,1)} %param.15, f32[12]{0:T(128)} %param.16), kind=kOutput, calls=%fused_computation.22 | convolution fusion | flops 18898944 | bytes 1658928 | tf_op jit(solution)/shard_map/dot_general | solution.py:231
  43.3 7.1 %convolution_convert_fusion = bf16[2304,2,128]{2,0,1:T(8,128)(2,1)S(1)} fusion(bf16[2304,3072,1]{1,0,2:T(8,128)(2,1)} %bitcast.33, bf16[2,128,3072]{2,1,0:T(8,128)(2,1)S(1)} %copy-done.1), kind=kOutput, calls=%fused_computation.9 | convolution fusion | flops 3624468480 | bytes 16908288 | tf_op jit(solution)/shard_map/dot_general | solution.py:227
  50.5 1.4 maximum_maximum_fusion
  51.9 5.2 %all-to-all-start = ((bf16[8,3,208,128]{3,2,1,0:T(8,128)(2,1)}), bf16[8,3,208,128]{3,2,1,0:T(8,128)(2,1)S(1)}, u32[]{:S(2)}, u32[]{:S(2)}) async-start(bf16[8,3,208,128]{3,2,1,0:T(8,128)(2,1)} %maximum_maximum_fusion), calls=%async_computation | async-start | bytes 2555904 | tf_op jit(solution)/shard_map/all_to_all | solution.py:245
  57.2 0.6 gather_fusion.1
  57.8 0.6 gather_fusion
  58.4 0.2 copy.16
  58.5 1.7 %gather_fusion.2 = f32[3,256,64]{1,2,0:T(8,128)S(1)} fusion(f32[12,256,64]{1,2,0:T(8,128)} %param.19, s32[1024]{0:T(1024)S(1)} %pad_clamp_fusion.1), kind=kCustom, calls=%fused_computation.5 | custom fusion | bytes 393228 | tf_op jit(solution)/shard_map/jit(_take)/gather | solution.py:180
  60.3 0.1 broadcast_select_fusion
  60.3 0.2 copy.17.second
  60.6 0.6 gather_fusion.5
  61.1 0.6 gather_fusion.4
  61.7 0.6 gather_fusion.3
  62.6 0.1 select_bitcast_fusion
  62.7 0.2 broadcast_in_dim.76
  62.8 0.2 maximum_maximum_fusion.1.first
  63.0 23.1 %all-to-all-done.x = bf16[8,3,208,128]{3,2,1,0:T(8,128)(2,1)S(1)} async-done(((bf16[8,3,208,128]{3,2,1,0:T(8,128)(2,1)}), bf16[8,3,208,128]{3,2,1,0:T(8,128)(2,1)S(1)}, u32[]{:S(2)}, u32[]{:S(2)}) %all-to-all-start) | async-done | bytes 1277984 | tf_op jit(solution)/shard_map/all_to_all | solution.py:245
  86.1 0.1 broadcast_in_dim.81.gain
  86.3 14.2 %shard_map.109 = bf16[8,3,64,128]{3,2,1,0:T(8,128)(2,1)S(1)} custom-call(bf16[8,3,208,128]{3,2,1,0:T(8,128)(2,1)S(1)} %all-to-all-done.x, f32[3,256,128]{2,1,0:T(8,128)S(1)} %maximum_maximum_fusion.1.first, f32[3,256,64]{2,1,0:T(8,128)S(1)} %copy.17.second, f32[3,64,256]{2,1,0:T(8,128)S(1)} %fusion.17.second_t, f32[3,64,128]{2,1,0:T(8,128)S(1)} %broadcast_in_dim.80.bias, ...), custom_call_target="tpu_custom_call" | custom-call | tf_op jit(solution)/shard_map/pallas_call | solution.py:156
  100.6 14.9 %all_to_all.10 = bf16[8,3,64,128]{3,2,1,0:T(8,128)(2,1)S(1)} all-to-all(bf16[8,3,64,128]{3,2,1,0:T(8,128)(2,1)S(1)} %shard_map.109), channel_id=1, replica_groups=mesh['seq'=8,'tensor'=4] {'seq'}, dimensions={0} | all-to-all | bytes 786432 | tf_op jit(solution)/shard_map/all_to_all | solution.py:249
  115.5 4.9 %fusion.2 = bf16[2,128,3072]{2,1,0:T(8,128)(2,1)} fusion(bf16[2,768,128]{2,1,0:T(8,128)(2,1)S(1)} %bitcast.31, bf16[768,3072]{1,0:T(8,128)(2,1)} %param.23), kind=kOutput, calls=%fused_computation.8 | convolution fusion | flops 1208745984 | bytes 6684672 | tf_op jit(solution)/shard_map/dot_general | solution.py:252
  120.5 31.1 %reduce-scatter.2.cloned.1.call-done = bf16[2,32,3072]{2,1,0:T(8,128)(2,1)} async-done(((bf16[2,128,3072]{2,1,0:T(8,128)(2,1)}), bf16[2,32,3072]{2,1,0:T(8,128)(2,1)}) %reduce-scatter.2.cloned.1.call-update) | async-done | bytes 393232 | tf_op jit(solution)/shard_map/reduce_scatter | solution.py:255
  (31 shorter events, 0.7 us)
Async XLA Ops:
  6.5 51.3 %copy-start = (f32[12,64,256]{2,1,0:T(8,128)S(1)}, f32[12,64,256]{2,1,0:T(8,128)}, u32[]{:S(2)}) copy-start(f32[12,64,256]{2,1,0:T(8,128)} %param.17) | copy-start | bytes 2359300
  6.5 34.7 %all-gather.2.cloned.1.call-start = ((), (), s32[]{:S(2)}) async-start(), calls=%async_computation.3 | async-start | bytes 1966080 | tf_op jit(solution)/shard_map/all_gather | solution.py:225
  41.2 2.1 %copy-start.1 = (bf16[2,128,3072]{2,1,0:T(8,128)(2,1)S(1)}, bf16[2,128,3072]{2,1,0:T(8,128)(2,1)}, u32[]{:S(2)}) copy-start(bf16[2,128,3072]{2,1,0:T(8,128)(2,1)} %all-gather.2.cloned.1.call-done) | copy-start | bytes 4718596
  51.9 5.3 %copy-start.2 = (f32[12,256]{1,0:T(8,128)S(1)}, f32[12,256]{1,0:T(8,128)}, u32[]{:S(2)}) copy-start(f32[12,256]{1,0:T(8,128)} %param.18) | copy-start | bytes 36868
  51.9 34.2 %all-to-all-start = ((bf16[8,3,208,128]{3,2,1,0:T(8,128)(2,1)}), bf16[8,3,208,128]{3,2,1,0:T(8,128)(2,1)S(1)}, u32[]{:S(2)}, u32[]{:S(2)}) async-start(bf16[8,3,208,128]{3,2,1,0:T(8,128)(2,1)} %maximum_maximum_fusion), calls=%async_computation | async-start | bytes 2555904 | tf_op jit(solution)/shard_map/all_to_all | solution.py:245
  57.1 3.4 %copy-start.3 = (f32[12,64]{1,0:T(8,128)S(1)}, f32[12,64]{1,0:T(8,128)}, u32[]{:S(2)}) copy-start(f32[12,64]{1,0:T(8,128)} %param.22) | copy-start | bytes 9220
  57.1 4.0 %copy-start.4 = (f32[12,64]{1,0:T(8,128)S(1)}, f32[12,64]{1,0:T(8,128)}, u32[]{:S(2)}) copy-start(f32[12,64]{1,0:T(8,128)} %param.21) | copy-start | bytes 9220
  57.1 4.6 %copy-start.5 = (f32[12,64]{1,0:T(8,128)S(1)}, f32[12,64]{1,0:T(8,128)}, u32[]{:S(2)}) copy-start(f32[12,64]{1,0:T(8,128)} %param.20) | copy-start | bytes 9220
  57.1 94.4 %reduce-scatter.2.cloned.1.call-start = ((), (), s32[]{:S(2)}) async-start(), calls=%async_computation.4 | async-start | bytes 1966080 | tf_op jit(solution)/shard_map/reduce_scatter | solution.py:255
Sparse Core Ops, SparseCore 0:
  9.2 31.9 all-gather.1
  120.6 30.9 reduce-scatter.1

commit v2 on v1

--- a/solution.py
+++ b/solution.py
@@ -11,11 +11,12 @@
 HEAD = 64
 MB = 64
 TILE = 128
-ROWS = 3 * HEAD + 16
+PAIRS = 8
 CURVE = math.sqrt(2.0 / math.pi)
 CUBIC = 0.044715
 F32 = jnp.float32
 BF16 = jnp.bfloat16
+MESH = pl.DeviceIdType.MESH
 NN = (((1,), (0,)), ((), ()))
 NT = (((1,), (1,)), ((), ()))
 
@@ -43,6 +44,11 @@
         w1b[c] = split_bias(first[c])
         w2b[c] = second[c].astype(BF16)
         w2tb[c] = second_t[c].astype(BF16)
+
+
+def rows_of(tile, chain, kind):
+    start = (3 * chain + kind) * HEAD
+    return tile[start : start + HEAD, :]
 
 
 def mini_batch(count, keys_low, learn, key_tile, query_tile, consts, state, bias2):
@@ -56,8 +62,8 @@
     rows = [
         jnp.where(
             is_key,
-            key_tile[c, HEAD : 2 * HEAD, :].astype(F32),
-            query_tile[c, :HEAD, :].astype(F32),
+            rows_of(key_tile, c, 1).astype(F32),
+            rows_of(query_tile, c, 0).astype(F32),
         )
         for c in each
     ]
@@ -75,7 +81,7 @@
     answer = [rows[c] + model[c] for c in each]
     if not learn:
         return answer
-    values = [key_tile[c, 2 * HEAD : 3 * HEAD, :].astype(F32) for c in each]
+    values = [rows_of(key_tile, c, 2).astype(F32) for c in each]
     upstream = [(model[c] - (values[c] - rows[c])) * gain[c] for c in each]
     grad_outer = [
         inverse[c]
@@ -87,9 +93,10 @@
         for c in each
     ]
     rates = []
+    tail = 3 * HEAD * count
+    pairs = key_tile[tail : tail + 2 * PAIRS, :].astype(F32)
     for c in each:
-        pair = key_tile[c, 3 * HEAD : 3 * HEAD + 16, :].astype(F32)
-        rate = pair[0:1, :] + pair[1:2, :]
+        rate = pairs[c : c + 1, :] + pairs[PAIRS + c : PAIRS + c + 1, :]
         rates.append(jnp.where(is_key[0:1, :], rate, 0.0))
     plain = [g.astype(BF16) for g in grad_outer]
     scaled_outer = [(rates[c] * grad_outer[c]).astype(BF16) for c in each]
@@ -116,8 +123,122 @@
     return answer
 
 
-def chain_kernel(tiles, count, x, first, second, second_t, bias, gain, shift, out,
-                 w1, w2, w2t, w1b, w2b, w2tb, bias2, low):
+def flipped(index, bits, count):
+    result = 0
+    place = 1
+    while place < count:
+        bit = lax.rem(index // place, 2)
+        result = result + place * ((1 - bit) if (bits // place) % 2 else bit)
+        place *= 2
+    return result
+
+
+def partner(index, step, count):
+    if count & (count - 1) == 0:
+        return flipped(index, step, count)
+    return lax.rem(index + step, count)
+
+
+def greet(axis, count):
+    me = lax.axis_index(axis)
+    barrier = pltpu.get_barrier_semaphore()
+    for step in range(1, count):
+        pl.semaphore_signal(
+            barrier, inc=1, device_id={axis: partner_all(me, step, count)}, device_id_type=MESH
+        )
+    pl.semaphore_wait(barrier, count - 1)
+    return me
+
+
+def partner_all(index, step, count):
+    return lax.rem(index + step, count)
+
+
+def gather_kernel(group, seqs, mine, out, send_sem, recv_sem, own_sem):
+    me = greet("tensor", group)
+    copies = []
+    for step in range(group - 1, 0, -1):
+        peer = partner(me, step, group)
+        for s in range(seqs):
+            copy = pltpu.make_async_remote_copy(
+                src_ref=mine.at[s],
+                dst_ref=out.at[s, me],
+                send_sem=send_sem.at[step, s],
+                recv_sem=recv_sem.at[s, me],
+                device_id={"tensor": peer},
+                device_id_type=MESH,
+            )
+            copy.start()
+            copies.append(copy)
+    own = [pltpu.make_async_copy(mine.at[s], out.at[s, me], own_sem.at[s]) for s in range(seqs)]
+    for copy in own:
+        copy.start()
+    for copy in own:
+        copy.wait()
+    for step in range(group - 1, 0, -1):
+        peer = partner(me, step, group)
+        for s in range(seqs):
+            pltpu.make_async_remote_copy(
+                src_ref=mine.at[s],
+                dst_ref=out.at[s, peer],
+                send_sem=send_sem.at[step, s],
+                recv_sem=recv_sem.at[s, peer],
+                device_id={"tensor": peer},
+                device_id_type=MESH,
+            ).wait_recv()
+    for copy in copies:
+        copy.wait_send()
+
+
+def gather_tokens(tokens):
+    group = lax.axis_size("tensor")
+    seqs, own, width = tokens.shape
+    spec = pl.BlockSpec(memory_space=pl.ANY)
+    out = pl.pallas_call(
+        functools.partial(gather_kernel, group, seqs),
+        out_shape=jax.ShapeDtypeStruct((seqs, group, own, width), BF16),
+        in_specs=[spec],
+        out_specs=spec,
+        scratch_shapes=[
+            pltpu.SemaphoreType.DMA((group, seqs)),
+            pltpu.SemaphoreType.DMA((seqs, group)),
+            pltpu.SemaphoreType.DMA((seqs,)),
+        ],
+        compiler_params=pltpu.CompilerParams(collective_id=1, has_side_effects=True),
+    )(tokens)
+    return out.reshape(seqs, group * own, width)
+
+
+def chain_kernel(places, parts, count, x, first, second, second_t, bias, gain, shift, back,
+                 w1, w2, w2t, w1b, w2b, w2tb, bias2, low, arrive, outs,
+                 send_sem, recv_sem, own_sem, back_send, back_recv, back_own):
+    me = greet("seq", places)
+
+    def forward(step, peer, source):
+        return pltpu.make_async_remote_copy(
+            src_ref=x.at[peer],
+            dst_ref=arrive.at[source],
+            send_sem=send_sem.at[step],
+            recv_sem=recv_sem.at[source],
+            device_id={"seq": peer},
+            device_id_type=MESH,
+        )
+
+    def homeward(place, source):
+        return pltpu.make_async_remote_copy(
+            src_ref=outs.at[place],
+            dst_ref=back.at[source],
+            send_sem=back_send.at[place],
+            recv_sem=back_recv.at[source],
+            device_id={"seq": place},
+            device_id_type=MESH,
+        )
+
+    for step in range(places - 1, 0, -1):
+        forward(step, partner(me, step, places), me).start()
+    own = pltpu.make_async_copy(x.at[me], arrive.at[me], own_sem)
+    own.start()
+    own_back = pltpu.make_async_copy(outs.at[me], back.at[me], back_own)
     state = (w1, w2, w2t, w1b, w2b, w2tb)
     load_state(count, first, second, second_t, state)
     bias2[...] = bias[...]
@@ -125,39 +246,73 @@
     consts = (gain, shift)
     lane = lax.broadcasted_iota(jnp.int32, (HEAD, TILE), 1)
 
-    def finish(tile, answer):
+    def finish(place, part, answer):
         for c in range(count):
-            out[tile, c] = jnp.where(lane < MB, low[c], answer[c]).astype(BF16)
-
-    def body(tile, carry):
-        before = jnp.maximum(tile - 1, 0)
-        answer = mini_batch(
-            count, True, True, x.at[tile], x.at[before], consts, state, bias2
-        )
-        finish(before, answer)
-        answer = mini_batch(
-            count, False, True, x.at[tile], x.at[tile], consts, state, bias2
-        )
-        for c in range(count):
-            low[c] = answer[c]
+            outs[place, part, c * HEAD : (c + 1) * HEAD, :] = jnp.where(
+                lane < MB, low[c], answer[c]
+            ).astype(BF16)
+
+    def send_home(place):
+        @pl.when(place == me)
+        def _():
+            own_back.start()
+
+        @pl.when(place != me)
+        def _():
+            homeward(place, me).start()
+
+    def body(place, carry):
+        @pl.when(place == me)
+        def _():
+            own.wait()
+
+        @pl.when(place != me)
+        def _():
+            forward(0, place, place).wait_recv()
+
+        for part in range(parts):
+            tile = arrive.at[place, part]
+            if part:
+                old_place, old_part = place, part - 1
+            else:
+                old_place, old_part = jnp.maximum(place - 1, 0), parts - 1
+            before = arrive.at[old_place, old_part]
+            answer = mini_batch(count, True, True, tile, before, consts, state, bias2)
+            finish(old_place, old_part, answer)
+            if not part:
+
+                @pl.when(place > 0)
+                def _():
+                    send_home(place - 1)
+
+            answer = mini_batch(count, False, True, tile, tile, consts, state, bias2)
+            for c in range(count):
+                low[c] = answer[c]
         return carry
 
-    lax.fori_loop(0, tiles, body, 0)
-    answer = mini_batch(
-        count, True, False, x.at[tiles - 1], x.at[tiles - 1], consts, state, bias2
-    )
-    finish(tiles - 1, answer)
-
-
-def run_chains(x, first, second, second_t, bias, gain, shift):
-    tiles, count = x.shape[:2]
+    lax.fori_loop(0, places, body, 0)
+    last = arrive.at[places - 1, parts - 1]
+    answer = mini_batch(count, True, False, last, last, consts, state, bias2)
+    finish(places - 1, parts - 1, answer)
+    send_home(places - 1)
+    own_back.wait()
+    for step in range(1, places):
+        peer = partner(me, step, places)
+        forward(step, peer, me).wait_send()
+        homeward(peer, peer).wait_recv()
+        homeward(peer, me).wait_send()
+
+
+def run_chains(x, count, first, second, second_t, bias, gain, shift):
+    places, parts, rows = x.shape[:3]
     inner = second.shape[1]
     vmem = pl.BlockSpec(memory_space=pltpu.VMEM)
+    whole = pl.BlockSpec(memory_space=pl.ANY)
     return pl.pallas_call(
-        functools.partial(chain_kernel, tiles, count),
-        out_shape=jax.ShapeDtypeStruct((tiles, count, HEAD, TILE), BF16),
-        in_specs=[vmem] * 7,
-        out_specs=vmem,
+        functools.partial(chain_kernel, places, parts, count),
+        out_shape=jax.ShapeDtypeStruct((places, parts, count * HEAD, TILE), BF16),
+        in_specs=[whole] + [vmem] * 6,
+        out_specs=whole,
         scratch_shapes=[
             pltpu.VMEM((count, inner, TILE), F32),
             pltpu.VMEM((count, inner, HEAD), F32),
@@ -167,9 +322,74 @@
             pltpu.VMEM((count, HEAD, inner), BF16),
             pltpu.VMEM((count, HEAD, TILE), F32),
             pltpu.VMEM((count, HEAD, TILE), F32),
+            pltpu.VMEM((places, parts, rows, TILE), BF16),
+            pltpu.VMEM((places, parts, count * HEAD, TILE), BF16),
+            pltpu.SemaphoreType.DMA((places,)),
+            pltpu.SemaphoreType.DMA((places,)),
+            pltpu.SemaphoreType.DMA,
+            pltpu.SemaphoreType.DMA((places,)),
+            pltpu.SemaphoreType.DMA((places,)),
+            pltpu.SemaphoreType.DMA,
         ],
-        compiler_params=pltpu.CompilerParams(vmem_limit_bytes=32 * 1024 * 1024),
+        compiler_params=pltpu.CompilerParams(
+            collective_id=2, has_side_effects=True, vmem_limit_bytes=32 * 1024 * 1024
+        ),
     )(x, first, second, second_t, bias, gain, shift)
+
+
+def mix_kernel(group, cuts, rows_ref, weight, out, ready, land, send_sem, recv_sem):
+    me = greet("tensor", group)
+    own, width = out.shape
+    piece = width // cuts
+
+    def move(cut, step, peer):
+        return pltpu.make_async_remote_copy(
+            src_ref=ready.at[cut, peer],
+            dst_ref=land.at[cut, step],
+            send_sem=send_sem.at[cut, step],
+            recv_sem=recv_sem.at[cut, step],
+            device_id={"tensor": peer},
+            device_id_type=MESH,
+        )
+
+    for cut in range(cuts):
+        part = dot(rows_ref[...], weight[:, cut * piece : (cut + 1) * piece])
+        ready[cut] = part.astype(BF16).reshape(group, own, piece)
+        for step in range(group - 1, 0, -1):
+            move(cut, step, partner(me, step, group)).start()
+    for cut in range(cuts):
+        total = ready[cut, me].astype(F32)
+        for step in range(group - 1, 0, -1):
+            move(cut, step, partner(me, step, group)).wait_recv()
+            total = total + land[cut, step].astype(F32)
+        out[:, cut * piece : (cut + 1) * piece] = total.astype(BF16)
+    for cut in range(cuts):
+        for step in range(group - 1, 0, -1):
+            move(cut, step, partner(me, step, group)).wait_send()
+
+
+def mix_heads(rows, weight):
+    group = lax.axis_size("tensor")
+    own = rows.shape[0] // group
+    width = weight.shape[1]
+    cuts = 6
+    piece = width // cuts
+    vmem = pl.BlockSpec(memory_space=pltpu.VMEM)
+    return pl.pallas_call(
+        functools.partial(mix_kernel, group, cuts),
+        out_shape=jax.ShapeDtypeStruct((own, width), BF16),
+        in_specs=[vmem, vmem],
+        out_specs=vmem,
+        scratch_shapes=[
+            pltpu.VMEM((cuts, group, own, piece), BF16),
+            pltpu.VMEM((cuts, group, own, piece), BF16),
+            pltpu.SemaphoreType.DMA((cuts, group)),
+            pltpu.SemaphoreType.DMA((cuts, group)),
+        ],
+        compiler_params=pltpu.CompilerParams(
+            collective_id=3, has_side_effects=True, vmem_limit_bytes=32 * 1024 * 1024
+        ),
+    )(rows, weight)
 
 
 def chain_params(heads, count, first_w, first_b, second_w, second_b, norm_gain, norm_shift, total):
@@ -219,40 +439,45 @@
     parts = block // TILE
     total = seqs * heads
     count = -(-total // places)
+    assert count <= PAIRS
     params = chain_params(
         heads, count, first_w, first_b, second_w, second_b, norm_gain, norm_shift, total
     )
-    piece = lax.all_gather(tokens, "tensor", axis=1, tiled=True)
+    piece = gather_tokens(tokens)
     contract = (((1,), (2,)), ((), ()))
     projected = lax.dot_general(
         qkv_weight.reshape(-1, width), piece, contract, preferred_element_type=F32
     ).astype(BF16)
     projected = projected.reshape(heads, 3 * HEAD, seqs, block).transpose(2, 0, 1, 3)
     logit = lax.dot_general(rate_weight, piece, contract, preferred_element_type=F32)
-    rates = (base_rate[:, None, None] * jax.nn.sigmoid(logit)).transpose(1, 0, 2)[:, :, None, :]
+    rates = (base_rate[:, None, None] * jax.nn.sigmoid(logit)).transpose(1, 0, 2)
+
+    def by_place(member):
+        member = member.reshape((total,) + member.shape[2:])
+        extra = places * count - total
+        if extra:
+            member = jnp.pad(member, ((0, extra),) + ((0, 0),) * (member.ndim - 1))
+        return member.reshape((places, -1, block))
+
     coarse = lax.reduce_precision(rates, 8, 7)
+    fill = jnp.zeros((places, PAIRS - count, block), BF16)
     load = jnp.concatenate(
         [
-            projected,
-            coarse.astype(BF16),
-            (rates - coarse).astype(BF16),
-            jnp.zeros((seqs, heads, 14, block), BF16),
+            by_place(projected),
+            by_place(coarse.astype(BF16)),
+            fill,
+            by_place((rates - coarse).astype(BF16)),
+            fill,
         ],
-        axis=2,
-    ).reshape(total, ROWS, block)
-    load = jnp.pad(load, ((0, places * count - total), (0, 0), (0, 0)))
-    load = load.reshape(places, count, ROWS, block)
-    arrived = lax.all_to_all(load, "seq", 0, 0)
-    arrived = arrived.reshape(places, count, ROWS, parts, TILE).transpose(0, 3, 1, 2, 4)
-    answers = run_chains(arrived.reshape(places * parts, count, ROWS, TILE), *params)
-    answers = answers.reshape(places, parts, count, HEAD, TILE).transpose(0, 2, 3, 1, 4)
-    answers = lax.all_to_all(answers.reshape(places, count, HEAD, block), "seq", 0, 0)
-    answers = answers.reshape(places * count, HEAD, block)[:total]
-    answers = answers.reshape(seqs, heads * HEAD, block)
-    partial = lax.dot_general(
-        answers, out_weight, (((1,), (0,)), ((), ())), preferred_element_type=F32
-    ).astype(BF16)
-    return lax.psum_scatter(partial, "tensor", scatter_dimension=1, tiled=True)
+        axis=1,
+    )
+    load = load.reshape(places, -1, parts, TILE).transpose(0, 2, 1, 3)
+    answers = run_chains(load, count, *params)
+    answers = answers.transpose(0, 2, 1, 3).reshape(places * count, HEAD, block)[:total]
+    group = lax.axis_size("tensor")
+    rows = answers.reshape(seqs, heads * HEAD, group, block // group)
+    rows = rows.transpose(2, 0, 3, 1).reshape(-1, heads * HEAD)
+    return mix_heads(rows, out_weight).reshape(tokens.shape)
 
 
 def solution(mesh):

time: 160 us -> 107 us (0.67)
  waiting for transfers between devices: 88.7 us -> 0 us
  Pallas kernels: 14.2 us -> 85.5 us
  blocking collectives: 14.9 us -> 0 us
  between operations: 13.6 us -> 0.27 us
  starting transfers between devices: 5.27 us -> 0 us
  local copies, waits for them, and re-layouts: 5.44 us -> 10.1 us
  matrix products: 14.1 us -> 10 us
    pallas_call x1 -> x3, Pallas kernels: 14.2 us -> 85.5 us  [the longest x1 43.1 us: run_chains(): pl.pallas_call(functools.partial(chain_kernel, places, parts, count), out...]
    all_gather x1 -> x0, waiting for transfers between devices: 33.8 us -> none  [shards(): piece = lax.all_gather(tokens, 'tensor', axis=1, tiled=True)]
    reduce_scatter x1 -> x0, waiting for transfers between devices: 31.1 us -> none  [shards(): return lax.psum_scatter(partial, 'tensor', scatter_dimension=1, tiled=True)]
    all_to_all x1 -> x0, waiting for transfers between devices: 23.1 us -> none  [shards(): arrived = lax.all_to_all(load, 'seq', 0, 0)]
    all_to_all x1 -> x0, blocking collectives: 14.9 us -> none  [shards(): lax.all_to_all(answers.reshape(places, count, HEAD, block), 'seq', 0, 0)]
    all_to_all x1 -> x0, starting transfers between devices: 5.23 us -> none  [shards(): arrived = lax.all_to_all(load, 'seq', 0, 0)]
    dot_general x1 -> x0, matrix products: 4.92 us -> none  [shards(): lax.dot_general(answers, out_weight, (((1,), (0,)), ((), ())), preferred_...]
    unnamed x12 -> x19, local copies, waits for them, and re-layouts: 0.02 us -> 3.3 us
  transfers between devices with their start and end apart: 3 -> 0, of which waited for: 3 -> 0; matrix products, arithmetic and copies ran while one was open for 4% -> 0% of each run, Pallas kernels for 0% -> 0%
where the time goes in v2:
time: 107 us
  Pallas kernels  85.5 us (80%)
  local copies, waits for them, and re-layouts  10.1 us (9%)
  matrix products  10 us (9%)
    pallas_call x1, Pallas kernels, run_chains(): pl.pallas_call(functools.partial(chain_kernel, places, parts, count), out...  43.1 us
    pallas_call x1, Pallas kernels, mix_heads(): pl.pallas_call(functools.partial(mix_kernel, group, cuts), out_shape=jax....  21.5 us
    pallas_call x1, Pallas kernels, gather_tokens(): pl.pallas_call(functools.partial(gather_kernel, group, seqs), out_shape=j...  20.8 us
    dot_general x1, matrix products, shards(): lax.dot_general(qkv_weight.reshape(-1, width), piece, contract, preferred...  9.48 us
    gather x7, local copies, waits for them, and re-layouts, pick(): return jnp.take(member, ids, axis=0)  4.66 us
    unnamed x19, local copies, waits for them, and re-layouts  3.3 us

profile of v2, /device:TPU:24, one launch (start us, length us, event | category | flops | bytes accessed | tf_op | source)
XLA Modules:
  0.0 106.6 jit_solution(9675926352804928925)
XLA Ops:
  0.0 20.8 %shard_map.109 = bf16[2,4,32,3072]{3,2,1,0:T(8,128)(2,1)} custom-call(bf16[2,32,3072]{2,1,0:T(8,128)(2,1)} %mine.1), custom_call_target="tpu_custom_call" | custom-call | tf_op jit(solution)/shard_map/pallas_call | solution.py:197
  20.8 9.5 %convolution_convert_fusion = bf16[2304,2,128]{2,0,1:T(8,128)(2,1)S(1)} fusion(bf16[2304,3072,1]{1,0,2:T(8,128)(2,1)} %bitcast.40, bf16[2,128,3072]{2,1,0:T(8,128)(2,1)} %bitcast.36), kind=kOutput, calls=%fused_computation.6 | convolution fusion | flops 3624468480 | bytes 16908288 | tf_op jit(solution)/shard_map/dot_general | solution.py:448
  30.4 0.5 fusion.6
  31.0 0.4 concatenate.6
  31.4 0.2 copy-done.4
  31.6 0.6 gather_fusion.1
  32.3 0.2 broadcast_in_dim.75
  32.5 0.6 gather_fusion
  33.0 0.2 copy.14
  33.2 0.1 select_bitcast_fusion
  33.4 0.2 maximum_maximum_fusion.first
  33.6 1.7 %gather_fusion.2 = f32[3,256,64]{1,2,0:T(8,128)S(1)} fusion(f32[12,256,64]{1,2,0:T(8,128)} %param.19, s32[1024]{0:T(1024)S(1)} %pad_clamp_fusion.1), kind=kCustom, calls=%fused_computation.5 | custom fusion | bytes 393228 | tf_op jit(solution)/shard_map/jit(_take)/gather | solution.py:400
  35.3 0.1 broadcast_select_fusion
  35.4 0.2 copy.15.second
  35.5 0.1 fusion.11.second_t
  35.7 0.6 gather_fusion.5
  36.2 0.6 gather_fusion.4
  36.8 0.6 gather_fusion.3
  37.7 43.1 %shard_map.110 = bf16[8,1,192,128]{3,2,1,0:T(8,128)(2,1)S(1)} custom-call(bf16[8,1,592,128]{3,2,1,0:T(8,128)(2,1)S(1)} %bitcast.33, f32[3,256,128]{2,1,0:T(8,128)S(1)} %maximum_maximum_fusion.first, f32[3,256,64]{2,1,0:T(8,128)S(1)} %copy.15.second, f32[3,64,256]{2,1,0:T(8,128)S(1)} %fusion.11.second_t, f32[3,64,128]{2,1,0:T(8,128)S(1)} %broadcast_in_dim.79.bias, ...), custom_call_target="tpu_custom_call" | custom-call | tf_op jit(solution)/shard_map/pallas_call | solution.py:311
  80.8 0.4 copy.16
  81.3 0.6 reshape_reshape_transpose.3
  81.9 2.3 %copy-done.1 = bf16[768,3072]{1,0:T(8,128)(2,1)S(1)} copy-done((bf16[768,3072]{1,0:T(8,128)(2,1)S(1)}, bf16[768,3072]{1,0:T(8,128)(2,1)}, u32[]{:S(2)}) %copy-start.1) | copy-done | bytes 4718616
  84.3 21.5 %shard_map.111 = bf16[64,3072]{1,0:T(8,128)(2,1)S(1)} custom-call(bf16[256,768]{1,0:T(8,128)(2,1)S(1)} %bitcast.34, bf16[768,3072]{1,0:T(8,128)(2,1)S(1)} %copy-done.1), custom_call_target="tpu_custom_call" | custom-call | tf_op jit(solution)/shard_map/pallas_call | solution.py:378
  105.8 0.7 copy.19
  (32 shorter events, 0.7 us)
Async XLA Ops:
  0.0 32.4 %copy-start = (f32[12,64,256]{2,1,0:T(8,128)S(1)}, f32[12,64,256]{2,1,0:T(8,128)}, u32[]{:S(2)}) copy-start(f32[12,64,256]{2,1,0:T(8,128)} %param.17) | copy-start | bytes 2359300
  20.8 9.5 %copy-start.2 = (bf16[2,4,32,3072]{3,2,1,0:T(8,128)(2,1)S(1)}, bf16[2,4,32,3072]{3,2,1,0:T(8,128)(2,1)}, u32[]{:S(2)}) copy-start(bf16[2,4,32,3072]{3,2,1,0:T(8,128)(2,1)} %shard_map.109) | copy-start | bytes 4718596
  20.8 9.5 %copy-start.3 = (bf16[12,3072]{1,0:T(8,128)(2,1)S(1)}, bf16[12,3072]{1,0:T(8,128)(2,1)}, u32[]{:S(2)}) copy-start(bf16[12,3072]{1,0:T(8,128)(2,1)} %param.15) | copy-start | bytes 221188
  20.8 9.5 %copy-start.8 = (f32[12]{0:T(128)S(1)}, f32[12]{0:T(128)}, u32[]{:S(2)}) copy-start(f32[12]{0:T(128)} %param.16) | copy-start | bytes 148
  30.9 0.7 copy-start.4
  33.4 2.3 %copy-start.5 = (f32[12,64]{1,0:T(8,128)S(1)}, f32[12,64]{1,0:T(8,128)}, u32[]{:S(2)}) copy-start(f32[12,64]{1,0:T(8,128)} %param.22) | copy-start | bytes 9220
  33.4 2.8 %copy-start.6 = (f32[12,64]{1,0:T(8,128)S(1)}, f32[12,64]{1,0:T(8,128)}, u32[]{:S(2)}) copy-start(f32[12,64]{1,0:T(8,128)} %param.21) | copy-start | bytes 9220
  33.4 3.4 %copy-start.7 = (f32[12,64]{1,0:T(8,128)S(1)}, f32[12,64]{1,0:T(8,128)}, u32[]{:S(2)}) copy-start(f32[12,64]{1,0:T(8,128)} %param.20) | copy-start | bytes 9220
  81.9 2.3 %copy-start.1 = (bf16[768,3072]{1,0:T(8,128)(2,1)S(1)}, bf16[768,3072]{1,0:T(8,128)(2,1)}, u32[]{:S(2)}) copy-start(bf16[768,3072]{1,0:T(8,128)(2,1)} %weight.1) | copy-start | bytes 14155780

commit v3 on v2

v3 whole, which is shorter than its diff:
```python
import functools
import math

import jax
import jax.numpy as jnp
from jax import lax
from jax.experimental import pallas as pl
from jax.experimental.pallas import tpu as pltpu
from jax.sharding import PartitionSpec as P

HEAD = 64
MB = 64
TILE = 128
PAIRS = 8
CURVE = math.sqrt(2.0 / math.pi)
CUBIC = 0.044715
F32 = jnp.float32
BF16 = jnp.bfloat16
MESH = pl.DeviceIdType.MESH
NN = (((1,), (0,)), ((), ()))
NT = (((1,), (1,)), ((), ()))


def dot(a, b, dims=NN):
    return lax.dot_general(a, b, dims, preferred_element_type=F32)


def split_bias(state):
    lane = lax.broadcasted_iota(jnp.int32, state.shape, 1)
    rest = state - state.astype(BF16).astype(F32)
    return jnp.where(lane == HEAD + 1, rest, state).astype(BF16)


def mean_rows(values):
    return jnp.sum(values, axis=0, keepdims=True) * (1.0 / HEAD)


def load_state(me, count, total, params, consts, state, bias2):
    first_w, first_b, second_w, second_b, norm_gain, norm_shift = params
    gain, shift = consts
    w1, w2, w2t, w1b, w2b, w2tb = state
    inner = first_w.shape[2]

    def column(member, head):
        return jnp.broadcast_to(member[head], (TILE, HEAD)).T

    for c in range(count):
        head = lax.rem(jnp.minimum(me * count + c, total - 1), first_w.shape[0])
        row = first_b[head]
        fill = jnp.zeros((TILE - HEAD - 2, inner), F32)
        first = jnp.concatenate([first_w[head], row, row, fill], axis=0).T
        second = second_w[head]
        w1[c] = first
        w1b[c] = split_bias(first)
        w2[c] = second
        w2b[c] = second.astype(BF16)
        w2t[c] = second.T
        w2tb[c] = second.T.astype(BF16)
        bias2[c] = column(second_b, head)
        gain[c] = column(norm_gain, head)
        shift[c] = column(norm_shift, head)


def rows_of(tile, chain, kind):
    start = (3 * chain + kind) * HEAD
    return tile[start : start + HEAD, :]


def mini_batch(count, keys_low, learn, key_tile, query_tile, consts, state, bias2):
    gain, shift = consts
    w1, w2, w2t, w1b, w2b, w2tb = state
    each = range(count)
    lane = lax.broadcasted_iota(jnp.int32, (HEAD, TILE), 1)
    is_key = (lane < MB) if keys_low else (lane >= MB)
    row = lax.broadcasted_iota(jnp.int32, (HEAD, TILE), 0)
    ones_rows = jnp.where(row < 2, 1.0, 0.0)
    rows = [
        jnp.where(
            is_key,
            rows_of(key_tile, c, 1).astype(F32),
            rows_of(query_tile, c, 0).astype(F32),
        )
        for c in each
    ]
    wide = [jnp.concatenate([rows[c], ones_rows], axis=0).astype(BF16) for c in each]
    pre = [dot(w1b[c], wide[c]) for c in each]
    square = [p * p for p in pre]
    bend = [jnp.tanh((CURVE * p) * (1.0 + CUBIC * s)) for p, s in zip(pre, square)]
    half = [0.5 + 0.5 * t for t in bend]
    hidden = [(p * h).astype(BF16) for p, h in zip(pre, half)]
    outer = [dot(w2tb[c], hidden[c]) + bias2[c] for c in each]
    centered = [o - mean_rows(o) for o in outer]
    inverse = [lax.rsqrt(mean_rows(z * z) + 1e-06) for z in centered]
    normed = [z * i for z, i in zip(centered, inverse)]
    model = [gain[c] * normed[c] + shift[c] for c in each]
    answer = [rows[c] + model[c] for c in each]
    if not learn:
        return answer
    values = [rows_of(key_tile, c, 2).astype(F32) for c in each]
    upstream = [(model[c] - (values[c] - rows[c])) * gain[c] for c in each]
    grad_outer = [
        inverse[c]
        * (
            upstream[c]
            - mean_rows(upstream[c])
            - normed[c] * mean_rows(upstream[c] * normed[c])
        )
        for c in each
    ]
    rates = []
    tail = 3 * HEAD * count
    pairs = key_tile[tail : tail + 2 * PAIRS, :].astype(F32)
    for c in each:
        rate = pairs[c : c + 1, :] + pairs[PAIRS + c : PAIRS + c + 1, :]
        rates.append(jnp.where(is_key[0:1, :], rate, 0.0))
    plain = [g.astype(BF16) for g in grad_outer]
    scaled_outer = [(rates[c] * grad_outer[c]).astype(BF16) for c in each]
    grad_hidden = [dot(w2b[c], plain[c]) for c in each]
    slope = [
        half[c]
        + (0.5 * CURVE) * pre[c] * (1.0 - bend[c] * bend[c]) * (1.0 + (3.0 * CUBIC) * square[c])
        for c in each
    ]
    scaled_inner = [(grad_hidden[c] * slope[c] * rates[c]).astype(BF16) for c in each]
    ones = jnp.ones((TILE, TILE), BF16)
    for c in each:
        new = w1[c] - dot(scaled_inner[c], wide[c], NT)
        w1[c] = new
        w1b[c] = split_bias(new)
    for c in each:
        new = w2t[c] - dot(scaled_outer[c], hidden[c], NT)
        w2t[c] = new
        w2tb[c] = new.astype(BF16)
        bias2[c] = bias2[c] - dot(scaled_outer[c], ones, NT)
        new = w2[c] - dot(hidden[c], scaled_outer[c], NT)
        w2[c] = new
        w2b[c] = new.astype(BF16)
    return answer


def flipped(index, bits, count):
    result = 0
    place = 1
    while place < count:
        bit = lax.rem(index // place, 2)
        result = result + place * ((1 - bit) if (bits // place) % 2 else bit)
        place *= 2
    return result


def partner(index, step, count):
    if count & (count - 1) == 0:
        return flipped(index, step, count)
    return lax.rem(index + step, count)


def greet(axes):
    barrier = pltpu.get_barrier_semaphore()
    for axis, count in axes:
        me = lax.axis_index(axis)
        for step in range(1, count):
            pl.semaphore_signal(
                barrier,
                inc=1,
                device_id={axis: lax.rem(me + step, count)},
                device_id_type=MESH,
            )
    pl.semaphore_wait(barrier, sum(count - 1 for _, count in axes))


def block_of(heads):
    return max(n for n in (4, 3, 2, 1) if heads % n == 0)


def project(sizes, group_me, mine, qkv, rate_weight, base, load, weights, sums, land,
            weight_sem, token_send, token_recv):
    places, group, seqs, heads, parts, count, own, pieces = sizes
    piece = mine.shape[1] // pieces
    total = seqs * heads
    block = group * own
    several = block_of(heads)

    def span(cut):
        return slice(cut * piece, (cut + 1) * piece)

    def fetch(cut):
        return pltpu.make_async_copy(
            qkv.at[:, span(cut)], weights.at[cut], weight_sem.at[cut]
        )

    def move(cut, step, peer, source):
        return pltpu.make_async_remote_copy(
            src_ref=mine.at[:, span(cut)],
            dst_ref=land.at[cut, source],
            send_sem=token_send.at[cut, step],
            recv_sem=token_recv.at[cut, source],
            device_id={"tensor": peer},
            device_id_type=MESH,
        )

    for cut in range(pieces):
        for step in range(group - 1, 0, -1):
            move(cut, step, partner(group_me, step, group), group_me).start()
    for cut in range(pieces):
        fetch(cut).start()
    yield
    logit = None
    for cut in range(pieces):
        land[cut, group_me] = mine[:, span(cut)]
        fetch(cut).wait()
        for step in range(group - 1, 0, -1):
            peer = partner(group_me, step, group)
            move(cut, step, peer, peer).wait_recv()
        wide = land[cut].astype(F32)
        tokens = jnp.concatenate(
            [wide[:, n * own : (n + 1) * own].reshape(block, piece) for n in range(seqs)], axis=0
        ).astype(BF16)
        more = dot(rate_weight[:, span(cut)], tokens, NT)
        logit = more if logit is None else logit + more

        def some_heads(index, carry):
            rows = pl.ds(pl.multiple_of(index * (several * 3 * HEAD), 64), several * 3 * HEAD)
            part = dot(weights[cut, rows, :], tokens, NT)
            part = part.reshape(several, 3 * HEAD, seqs * block)
            at = pl.ds(index * several, several)
            sums[at] = part if cut == 0 else sums[at] + part
            return carry

        lax.fori_loop(0, heads // several, some_heads, 0)
    if places * count > total:
        load[...] = jnp.zeros_like(load)
    rates = base[...][:, :1] * jax.nn.sigmoid(logit)
    for place in range(places):
        for part in range(parts):
            coarse, fine = [], []
            for c in range(count):
                chain = place * count + c
                if chain >= total:
                    break
                n, head = chain // heads, chain % heads
                lanes = slice(n * block + part * TILE, n * block + (part + 1) * TILE)
                load[place, part, c * 3 * HEAD : (c + 1) * 3 * HEAD, :] = sums[
                    head, :, lanes
                ].astype(BF16)
                row = rates[head : head + 1, lanes]
                short = row.astype(BF16).astype(F32)
                coarse.append(short)
                fine.append(row - short)
            if coarse:
                fill = [jnp.zeros((PAIRS - len(coarse), TILE), F32)]
                load[place, part, count * 3 * HEAD :, :] = jnp.concatenate(
                    coarse + fill + fine + fill, axis=0
                ).astype(BF16)
    for cut in range(pieces):
        for step in range(group - 1, 0, -1):
            move(cut, step, partner(group_me, step, group), group_me).wait_send()


def layer_kernel(sizes, mine, qkv, rate_weight, base, first_w, first_b, second_w, second_b,
                 norm_gain, norm_shift, mix_weight, out,
                 w1, w2, w2t, w1b, w2b, w2tb, bias2, low, gain, shift,
                 x, arrive, outs, back, weights, sums, land, mix, ready, shares,
                 weight_sem, token_send, token_recv, mix_sem,
                 send_sem, recv_sem, own_sem, back_send, back_recv, back_own,
                 share_send, share_recv):
    places, group, seqs, heads, parts, count, own_rows, pieces = sizes
    total_chains = seqs * heads
    me = lax.axis_index("seq")
    group_me = lax.axis_index("tensor")
    greet((("tensor", group), ("seq", places)))
    front = project(
        sizes, group_me, mine, qkv, rate_weight, base, x, weights, sums, land,
        weight_sem, token_send, token_recv,
    )
    next(front)
    mix_copy = pltpu.make_async_copy(mix_weight, mix, mix_sem)
    mix_copy.start()
    state = (w1, w2, w2t, w1b, w2b, w2tb)
    consts = (gain, shift)
    params = (first_w, first_b, second_w, second_b, norm_gain, norm_shift)
    load_state(me, count, total_chains, params, consts, state, bias2)
    low[...] = jnp.zeros_like(low)
    for _ in front:
        pass

    def forward(step, peer, source):
        return pltpu.make_async_remote_copy(
            src_ref=x.at[peer],
            dst_ref=arrive.at[source],
            send_sem=send_sem.at[step],
            recv_sem=recv_sem.at[source],
            device_id={"seq": peer},
            device_id_type=MESH,
        )

    def homeward(place, source):
        return pltpu.make_async_remote_copy(
            src_ref=outs.at[place],
            dst_ref=back.at[source],
            send_sem=back_send.at[place],
            recv_sem=back_recv.at[source],
            device_id={"seq": place},
            device_id_type=MESH,
        )

    for step in range(places - 1, 0, -1):
        forward(step, partner(me, step, places), me).start()
    own = pltpu.make_async_copy(x.at[me], arrive.at[me], own_sem)
    own.start()
    own_back = pltpu.make_async_copy(outs.at[me], back.at[me], back_own)
    lane = lax.broadcasted_iota(jnp.int32, (HEAD, TILE), 1)

    def finish(place, part, answer):
        for c in range(count):
            outs[place, part, c * HEAD : (c + 1) * HEAD, :] = jnp.where(
                lane < MB, low[c], answer[c]
            ).astype(BF16)

    def send_home(place):
        @pl.when(place == me)
        def _():
            own_back.start()

        @pl.when(place != me)
        def _():
            homeward(place, me).start()

    def body(place, carry):
        @pl.when(place == me)
        def _():
            own.wait()

        @pl.when(place != me)
        def _():
            forward(0, place, place).wait_recv()

        for part in range(parts):
            tile = arrive.at[place, part]
            if part:
                old_place, old_part = place, part - 1
            else:
                old_place, old_part = jnp.maximum(place - 1, 0), parts - 1
            before = arrive.at[old_place, old_part]
            answer = mini_batch(count, True, True, tile, before, consts, state, bias2)
            finish(old_place, old_part, answer)
            if not part:

                @pl.when(place > 0)
                def _():
                    send_home(place - 1)

            answer = mini_batch(count, False, True, tile, tile, consts, state, bias2)
            for c in range(count):
                low[c] = answer[c]
        return carry

    lax.fori_loop(0, places, body, 0)
    last = arrive.at[places - 1, parts - 1]
    answer = mini_batch(count, True, False, last, last, consts, state, bias2)
    finish(places - 1, parts - 1, answer)
    send_home(places - 1)
    own_back.wait()
    for step in range(1, places):
        peer = partner(me, step, places)
        forward(step, peer, me).wait_send()
        homeward(peer, peer).wait_recv()
        homeward(peer, me).wait_send()


    mix_copy.wait()
    flat = back[...]
    flat = jnp.concatenate(
        [flat[:, part].reshape(places * count * HEAD, TILE) for part in range(parts)], axis=1
    )
    feats = heads * HEAD
    rows = [flat[n * feats : (n + 1) * feats].astype(F32).T.astype(BF16) for n in range(seqs)]
    width = mix.shape[1]
    cuts = ready.shape[0]
    piece = width // cuts

    def move(cut, step, peer):
        return pltpu.make_async_remote_copy(
            src_ref=ready.at[cut, peer],
            dst_ref=shares.at[cut, step],
            send_sem=share_send.at[cut, step],
            recv_sem=share_recv.at[cut, step],
            device_id={"tensor": peer},
            device_id_type=MESH,
        )

    both = jnp.concatenate(rows, axis=0)
    for cut in range(cuts):
        part = dot(both, mix[:, cut * piece : (cut + 1) * piece])
        part = part.reshape(seqs, group, own_rows, piece)
        ready[cut] = jnp.concatenate([part[n] for n in range(seqs)], axis=1).astype(BF16)
        for step in range(group - 1, 0, -1):
            move(cut, step, partner(group_me, step, group)).start()
    for cut in range(cuts):
        result = ready[cut, group_me].astype(F32)
        for step in range(group - 1, 0, -1):
            move(cut, step, partner(group_me, step, group)).wait_recv()
            result = result + shares[cut, step].astype(F32)
        out[:, cut * piece : (cut + 1) * piece] = result.astype(BF16)
    for cut in range(cuts):
        for step in range(group - 1, 0, -1):
            move(cut, step, partner(group_me, step, group)).wait_send()


def shards(
    tokens,
    qkv_weight,
    rate_weight,
    base_rate,
    first_w,
    first_b,
    second_w,
    second_b,
    norm_gain,
    norm_shift,
    out_weight,
):
    places = lax.axis_size("seq")
    group = lax.axis_size("tensor")
    seqs, own, width = tokens.shape
    block = own * group
    heads, _, inner = first_w.shape
    assert block % TILE == 0
    parts = block // TILE
    count = -(-seqs * heads // places)
    assert count <= PAIRS
    pieces = cuts = 6
    piece = width // pieces
    sizes = (places, group, seqs, heads, parts, count, own, pieces)
    vmem = pl.BlockSpec(memory_space=pltpu.VMEM)
    whole = pl.BlockSpec(memory_space=pl.ANY)
    dma = pltpu.SemaphoreType.DMA
    rows = count * 3 * HEAD + 2 * PAIRS
    out = pl.pallas_call(
        functools.partial(layer_kernel, sizes),
        out_shape=jax.ShapeDtypeStruct((seqs * own, width), BF16),
        in_specs=[vmem, whole] + [vmem] * 8 + [whole],
        out_specs=vmem,
        scratch_shapes=[
            pltpu.VMEM((count, inner, TILE), F32),
            pltpu.VMEM((count, inner, HEAD), F32),
            pltpu.VMEM((count, HEAD, inner), F32),
            pltpu.VMEM((count, inner, TILE), BF16),
            pltpu.VMEM((count, inner, HEAD), BF16),
            pltpu.VMEM((count, HEAD, inner), BF16),
            pltpu.VMEM((count, HEAD, TILE), F32),
            pltpu.VMEM((count, HEAD, TILE), F32),
            pltpu.VMEM((count, HEAD, TILE), F32),
            pltpu.VMEM((count, HEAD, TILE), F32),
            pltpu.VMEM((places, parts, rows, TILE), BF16),
            pltpu.VMEM((places, parts, rows, TILE), BF16),
            pltpu.VMEM((places, parts, count * HEAD, TILE), BF16),
            pltpu.VMEM((places, parts, count * HEAD, TILE), BF16),
            pltpu.VMEM((pieces, heads * 3 * HEAD, piece), BF16),
            pltpu.VMEM((heads, 3 * HEAD, seqs * block), F32),
            pltpu.VMEM((pieces, group, seqs * own, piece), BF16),
            pltpu.VMEM((heads * HEAD, width), BF16),
            pltpu.VMEM((cuts, group, seqs * own, width // cuts), BF16),
            pltpu.VMEM((cuts, group, seqs * own, width // cuts), BF16),
            dma((pieces,)),
            dma((pieces, group)),
            dma((pieces, group)),
            dma,
            dma((places,)),
            dma((places,)),
            dma,
            dma((places,)),
            dma((places,)),
            dma,
            dma((cuts, group)),
            dma((cuts, group)),
        ],
        compiler_params=pltpu.CompilerParams(
            collective_id=1, has_side_effects=True, vmem_limit_bytes=56 * 1024 * 1024
        ),
    )(
        tokens.reshape(seqs * own, width),
        qkv_weight.reshape(-1, width),
        rate_weight,
        jnp.broadcast_to(base_rate[:, None], (heads, TILE)),
        first_w,
        first_b[:, None],
        second_w,
        second_b[:, None],
        norm_gain[:, None],
        norm_shift[:, None],
        out_weight,
    )
    return out.reshape(tokens.shape)


def solution(mesh):
    in_specs = (
        P(None, ("seq", "tensor"), None),
        P("tensor", None, None),
        P("tensor", None),
        P("tensor"),
        P("tensor", None, None),
        P("tensor", None),
        P("tensor", None, None),
        P("tensor", None),
        P("tensor", None),
        P("tensor", None),
        P("tensor", None),
    )
    out_specs = P(None, ("seq", "tensor"), None)
    return jax.shard_map(shards, mesh=mesh, in_specs=in_specs, out_specs=out_specs, check_vma=False)
```

time: 107 us -> 99.1 us (0.926)
  matrix products: 10 us -> 0 us
  Pallas kernels: 85.5 us -> 87.4 us
    dot_general x2 -> x0, matrix products: 10 us -> none  [the longest x1 9.48 us: shards(): lax.dot_general(qkv_weight.reshape(-1, width), piece, contract, preferred...]
    broadcast_in_dim x6 -> x5, local copies, waits for them, and re-layouts: 0.42 us -> 6.51 us  [the longest x1 1.32 us: shards(): first_b[:, None]]
    gather x7 -> x0, local copies, waits for them, and re-layouts: 4.66 us -> none  [pick(): return jnp.take(member, ids, axis=0)]
    pallas_call x3 -> x1, Pallas kernels: 85.5 us -> 87.4 us  [shards(): pl.pallas_call(functools.partial(layer_kernel, sizes), out_shape=jax.Shap...]
    unnamed x19 -> x2, local copies, waits for them, and re-layouts: 3.3 us -> 4.53 us
where the time goes in v3:
time: 99.1 us; the launch traced here: 98.4 us
  Pallas kernels  87.4 us (88%)
  local copies, waits for them, and re-layouts  11 us (11%)
    pallas_call x1, Pallas kernels, shards(): pl.pallas_call(functools.partial(layer_kernel, sizes), out_shape=jax.Shap...  87.4 us
    unnamed x2, local copies, waits for them, and re-layouts  4.53 us

profile of v3, /device:TPU:24, one launch (start us, length us, event | category | flops | bytes accessed | tf_op | source)
XLA Modules:
  0.0 98.4 jit_solution(1069123913990304221)
XLA Ops:
  0.0 1.3 %broadcast_in_dim.20.second_b = f32[12,1,64]{2,1,0:T(1,128)} reshape(f32[12,64]{1,0:T(8,128)} %param.18) | data formatting | bytes 6144 | tf_op jit(solution)/shard_map/broadcast_in_dim | solution.py:488
  1.3 1.3 %broadcast_in_dim.21.norm_gain = f32[12,1,64]{2,1,0:T(1,128)} reshape(f32[12,64]{1,0:T(8,128)} %param.19) | data formatting | bytes 6144 | tf_op jit(solution)/shard_map/broadcast_in_dim | solution.py:489
  2.6 1.3 %broadcast_in_dim.22.norm_shift = f32[12,1,64]{2,1,0:T(1,128)} reshape(f32[12,64]{1,0:T(8,128)} %param.20) | data formatting | bytes 6144 | tf_op jit(solution)/shard_map/broadcast_in_dim | solution.py:490
  3.9 1.3 %broadcast_in_dim.18.base = f32[12,128]{1,0:T(8,128)} broadcast(f32[12]{0:T(128)} %param.14), dimensions={0} | broadcast | bytes 6192 | tf_op jit(solution)/shard_map/broadcast_in_dim | solution.py:484
  5.2 1.3 %broadcast_in_dim.19.first_b = f32[12,1,256]{2,1,0:T(1,128)} reshape(f32[12,256]{1,0:T(8,128)} %param.16) | data formatting | bytes 24576 | tf_op jit(solution)/shard_map/broadcast_in_dim | solution.py:486
  6.5 2.8 %copy.12.second_w = f32[12,256,64]{2,1,0:T(8,128)} copy(f32[12,256,64]{1,2,0:T(8,128)} %param.17) | data formatting | bytes 1572864 | tf_op args[6]
  9.3 87.4 %shard_map.109 = bf16[64,3072]{1,0:T(8,128)(2,1)} custom-call(bf16[64,3072]{1,0:T(8,128)(2,1)} %bitcast.5, bf16[2304,3072]{1,0:T(8,128)(2,1)} %bitcast.3, bf16[12,3072]{1,0:T(8,128)(2,1)} %rate_weight.1, f32[12,128]{1,0:T(8,128)} %broadcast_in_dim.18.base, f32[12,64,256]{2,1,0:T(8,128)} %first_w.1, f32[12,1,256]{2,1,0:T(1,128)} %broadcast_in_dim.19.first_b, ...), custom_call_target="tpu_custom_call" | custom-call | tf_op jit(solution)/shard_map/pallas_call | solution.py:438
  96.7 1.8 %copy.14 = bf16[2,32,3072]{2,1,0:T(8,128)(2,1)} copy(bf16[2,32,3072]{2,1,0:T(8,128)(2,1)} %bitcast.4) | data formatting | bytes 786432

commit v4 on v3

--- a/solution.py
+++ b/solution.py
@@ -41,29 +41,33 @@
     w1, w2, w2t, w1b, w2b, w2tb = state
     inner = first_w.shape[2]
 
+    def one(member, head):
+        return member[pl.ds(head, 1), :]
+
     def column(member, head):
-        return jnp.broadcast_to(member[head], (TILE, HEAD)).T
+        return jnp.broadcast_to(one(member, head), (TILE, HEAD)).T
 
     for c in range(count):
-        head = lax.rem(jnp.minimum(me * count + c, total - 1), first_w.shape[0])
-        row = first_b[head]
+        head = jnp.minimum(me * count + c, total - 1) // (total // first_w.shape[0])
+        row = one(first_b, head)
         fill = jnp.zeros((TILE - HEAD - 2, inner), F32)
         first = jnp.concatenate([first_w[head], row, row, fill], axis=0).T
-        second = second_w[head]
+        second_t = second_w[head]
+        second = second_t.T
         w1[c] = first
         w1b[c] = split_bias(first)
         w2[c] = second
         w2b[c] = second.astype(BF16)
-        w2t[c] = second.T
-        w2tb[c] = second.T.astype(BF16)
+        w2t[c] = second_t
+        w2tb[c] = second_t.astype(BF16)
         bias2[c] = column(second_b, head)
         gain[c] = column(norm_gain, head)
         shift[c] = column(norm_shift, head)
 
 
 def rows_of(tile, chain, kind):
-    start = (3 * chain + kind) * HEAD
-    return tile[start : start + HEAD, :]
+    chains, _, part = tile
+    return chains[chain, part, kind * HEAD : (kind + 1) * HEAD, :]
 
 
 def mini_batch(count, keys_low, learn, key_tile, query_tile, consts, state, bias2):
@@ -108,8 +112,7 @@
         for c in each
     ]
     rates = []
-    tail = 3 * HEAD * count
-    pairs = key_tile[tail : tail + 2 * PAIRS, :].astype(F32)
+    pairs = key_tile[1][key_tile[2]].astype(F32)
     for c in each:
         rate = pairs[c : c + 1, :] + pairs[PAIRS + c : PAIRS + c + 1, :]
         rates.append(jnp.where(is_key[0:1, :], rate, 0.0))
@@ -172,10 +175,10 @@
     return max(n for n in (4, 3, 2, 1) if heads % n == 0)
 
 
-def project(sizes, group_me, mine, qkv, rate_weight, base, load, weights, sums, land,
-            weight_sem, token_send, token_recv):
+def project(sizes, group_me, mine, qkv, rate_weight, base, load, load_rates, weights, sums,
+            land, weight_sem, token_send, token_recv, between, ready):
     places, group, seqs, heads, parts, count, own, pieces = sizes
-    piece = mine.shape[1] // pieces
+    piece = mine.shape[2] // pieces
     total = seqs * heads
     block = group * own
     several = block_of(heads)
@@ -188,78 +191,84 @@
             qkv.at[:, span(cut)], weights.at[cut], weight_sem.at[cut]
         )
 
-    def move(cut, step, peer, source):
+    def move(n, cut, step, peer, source):
         return pltpu.make_async_remote_copy(
-            src_ref=mine.at[:, span(cut)],
-            dst_ref=land.at[cut, source],
-            send_sem=token_send.at[cut, step],
-            recv_sem=token_recv.at[cut, source],
+            src_ref=mine.at[n, :, span(cut)],
+            dst_ref=land.at[n, cut, source],
+            send_sem=token_send.at[n, cut, step],
+            recv_sem=token_recv.at[n, cut, source],
             device_id={"tensor": peer},
             device_id_type=MESH,
         )
 
-    for cut in range(pieces):
-        for step in range(group - 1, 0, -1):
-            move(cut, step, partner(group_me, step, group), group_me).start()
+    for n in range(seqs):
+        for cut in range(pieces):
+            for step in range(group - 1, 0, -1):
+                move(n, cut, step, partner(group_me, step, group), group_me).start()
     for cut in range(pieces):
         fetch(cut).start()
-    yield
-    logit = None
-    for cut in range(pieces):
-        land[cut, group_me] = mine[:, span(cut)]
-        fetch(cut).wait()
-        for step in range(group - 1, 0, -1):
-            peer = partner(group_me, step, group)
-            move(cut, step, peer, peer).wait_recv()
-        wide = land[cut].astype(F32)
-        tokens = jnp.concatenate(
-            [wide[:, n * own : (n + 1) * own].reshape(block, piece) for n in range(seqs)], axis=0
-        ).astype(BF16)
-        more = dot(rate_weight[:, span(cut)], tokens, NT)
-        logit = more if logit is None else logit + more
-
-        def some_heads(index, carry):
-            rows = pl.ds(pl.multiple_of(index * (several * 3 * HEAD), 64), several * 3 * HEAD)
-            part = dot(weights[cut, rows, :], tokens, NT)
-            part = part.reshape(several, 3 * HEAD, seqs * block)
-            at = pl.ds(index * several, several)
-            sums[at] = part if cut == 0 else sums[at] + part
-            return carry
-
-        lax.fori_loop(0, heads // several, some_heads, 0)
     if places * count > total:
         load[...] = jnp.zeros_like(load)
-    rates = base[...][:, :1] * jax.nn.sigmoid(logit)
+    between()
+    gates = []
+    for n in range(seqs):
+        logit = None
+        for cut in range(pieces):
+            land[n, cut, group_me] = mine[n, :, span(cut)]
+            if n == 0:
+                fetch(cut).wait()
+            for step in range(group - 1, 0, -1):
+                peer = partner(group_me, step, group)
+                move(n, cut, step, peer, peer).wait_recv()
+            tokens = land[n, cut].astype(F32).reshape(block, piece).astype(BF16)
+            more = dot(rate_weight[:, span(cut)], tokens, NT)
+            logit = more if logit is None else logit + more
+
+            def some_heads(index, carry):
+                start = pl.multiple_of(index * (several * 3 * HEAD), 64)
+                rows = pl.ds(start, several * 3 * HEAD)
+                part = dot(weights[cut, rows, :], tokens, NT)
+                part = part.reshape(several, 3 * HEAD, block)
+                at = pl.ds(index * several, several)
+                sums[at] = part if cut == 0 else sums[at] + part
+                return carry
+
+            lax.fori_loop(0, heads // several, some_heads, 0)
+        gates.append(jax.nn.sigmoid(logit))
+        for head in range(heads):
+            place, c = divmod(head * seqs + n, count)
+            for part in range(parts):
+                load[place, c, part] = sums[head, :, part * TILE : (part + 1) * TILE].astype(BF16)
+        if n + 1 < seqs:
+            ready(n)
     for place in range(places):
         for part in range(parts):
             coarse, fine = [], []
             for c in range(count):
-                chain = place * count + c
-                if chain >= total:
-                    break
-                n, head = chain // heads, chain % heads
-                lanes = slice(n * block + part * TILE, n * block + (part + 1) * TILE)
-                load[place, part, c * 3 * HEAD : (c + 1) * 3 * HEAD, :] = sums[
-                    head, :, lanes
-                ].astype(BF16)
-                row = rates[head : head + 1, lanes]
+                head, n = divmod(min(place * count + c, total - 1), seqs)
+                row = base[head] * gates[n][head : head + 1, part * TILE : (part + 1) * TILE]
                 short = row.astype(BF16).astype(F32)
                 coarse.append(short)
                 fine.append(row - short)
-            if coarse:
-                fill = [jnp.zeros((PAIRS - len(coarse), TILE), F32)]
-                load[place, part, count * 3 * HEAD :, :] = jnp.concatenate(
-                    coarse + fill + fine + fill, axis=0
-                ).astype(BF16)
-    for cut in range(pieces):
-        for step in range(group - 1, 0, -1):
-            move(cut, step, partner(group_me, step, group), group_me).wait_send()
+            fill = [jnp.zeros((PAIRS - count, TILE), F32)] if count < PAIRS else []
+            load_rates[place, part] = jnp.concatenate(
+                coarse + fill + fine + fill, axis=0
+            ).astype(BF16)
+    ready(seqs - 1)
+
+    def drain():
+        for n in range(seqs):
+            for cut in range(pieces):
+                for step in range(group - 1, 0, -1):
+                    move(n, cut, step, partner(group_me, step, group), group_me).wait_send()
+
+    return drain
 
 
 def layer_kernel(sizes, mine, qkv, rate_weight, base, first_w, first_b, second_w, second_b,
                  norm_gain, norm_shift, mix_weight, out,
                  w1, w2, w2t, w1b, w2b, w2tb, bias2, low, gain, shift,
-                 x, arrive, outs, back, weights, sums, land, mix, ready, shares,
+                 x, x_rates, arrive, arrive_rates, outs, back, weights, sums, land, mix, ready, shares,
                  weight_sem, token_send, token_recv, mix_sem,
                  send_sem, recv_sem, own_sem, back_send, back_recv, back_own,
                  share_send, share_recv):
@@ -268,27 +277,23 @@
     me = lax.axis_index("seq")
     group_me = lax.axis_index("tensor")
     greet((("tensor", group), ("seq", places)))
-    front = project(
-        sizes, group_me, mine, qkv, rate_weight, base, x, weights, sums, land,
-        weight_sem, token_send, token_recv,
-    )
-    next(front)
-    mix_copy = pltpu.make_async_copy(mix_weight, mix, mix_sem)
-    mix_copy.start()
-    state = (w1, w2, w2t, w1b, w2b, w2tb)
-    consts = (gain, shift)
-    params = (first_w, first_b, second_w, second_b, norm_gain, norm_shift)
-    load_state(me, count, total_chains, params, consts, state, bias2)
-    low[...] = jnp.zeros_like(low)
-    for _ in front:
-        pass
-
-    def forward(step, peer, source):
+
+    def forward(step, c, peer, source):
         return pltpu.make_async_remote_copy(
-            src_ref=x.at[peer],
-            dst_ref=arrive.at[source],
-            send_sem=send_sem.at[step],
-            recv_sem=recv_sem.at[source],
+            src_ref=x.at[peer, c],
+            dst_ref=arrive.at[source, c],
+            send_sem=send_sem.at[step, c],
+            recv_sem=recv_sem.at[source, c],
+            device_id={"seq": peer},
+            device_id_type=MESH,
+        )
+
+    def forward_rates(step, peer, source):
+        return pltpu.make_async_remote_copy(
+            src_ref=x_rates.at[peer],
+            dst_ref=arrive_rates.at[source],
+            send_sem=send_sem.at[step, count],
+            recv_sem=recv_sem.at[source, count],
             device_id={"seq": peer},
             device_id_type=MESH,
         )
@@ -303,11 +308,37 @@
             device_id_type=MESH,
         )
 
-    for step in range(places - 1, 0, -1):
-        forward(step, partner(me, step, places), me).start()
-    own = pltpu.make_async_copy(x.at[me], arrive.at[me], own_sem)
-    own.start()
+    own = pltpu.make_async_copy(x.at[me], arrive.at[me], own_sem.at[0])
+    own_rates = pltpu.make_async_copy(x_rates.at[me], arrive_rates.at[me], own_sem.at[1])
     own_back = pltpu.make_async_copy(outs.at[me], back.at[me], back_own)
+    mix_copy = pltpu.make_async_copy(mix_weight, mix, mix_sem)
+    state = (w1, w2, w2t, w1b, w2b, w2tb)
+    consts = (gain, shift)
+    params = (first_w, first_b, second_w, second_b, norm_gain, norm_shift)
+
+    def between():
+        mix_copy.start()
+        load_state(me, count, total_chains, params, consts, state, bias2)
+        low[...] = jnp.zeros_like(low)
+
+    def ready_rows(n):
+        if n == seqs - 1:
+            for step in range(places - 1, 0, -1):
+                forward_rates(step, partner(me, step, places), me).start()
+            own.start()
+            own_rates.start()
+        for step in range(places - 1, 0, -1):
+            peer = partner(me, step, places)
+            for c in range(count):
+
+                @pl.when(lax.rem(peer * count + c, seqs) == n)
+                def _():
+                    forward(step, c, peer, me).start()
+
+    drain = project(
+        sizes, group_me, mine, qkv, rate_weight, base, x, x_rates, weights, sums, land,
+        weight_sem, token_send, token_recv, between, ready_rows,
+    )
     lane = lax.broadcasted_iota(jnp.int32, (HEAD, TILE), 1)
 
     def finish(place, part, answer):
@@ -329,18 +360,21 @@
         @pl.when(place == me)
         def _():
             own.wait()
+            own_rates.wait()
 
         @pl.when(place != me)
         def _():
-            forward(0, place, place).wait_recv()
+            forward_rates(0, place, place).wait_recv()
+            for c in range(count):
+                forward(0, c, place, place).wait_recv()
 
         for part in range(parts):
-            tile = arrive.at[place, part]
+            tile = (arrive.at[place], arrive_rates.at[place], part)
             if part:
                 old_place, old_part = place, part - 1
             else:
                 old_place, old_part = jnp.maximum(place - 1, 0), parts - 1
-            before = arrive.at[old_place, old_part]
+            before = (arrive.at[old_place], None, old_part)
             answer = mini_batch(count, True, True, tile, before, consts, state, bias2)
             finish(old_place, old_part, answer)
             if not part:
@@ -355,25 +389,33 @@
         return carry
 
     lax.fori_loop(0, places, body, 0)
-    last = arrive.at[places - 1, parts - 1]
+    last = (arrive.at[places - 1], None, parts - 1)
     answer = mini_batch(count, True, False, last, last, consts, state, bias2)
     finish(places - 1, parts - 1, answer)
     send_home(places - 1)
     own_back.wait()
     for step in range(1, places):
         peer = partner(me, step, places)
-        forward(step, peer, me).wait_send()
+        forward_rates(step, peer, me).wait_send()
+        for c in range(count):
+            forward(step, c, peer, me).wait_send()
         homeward(peer, peer).wait_recv()
         homeward(peer, me).wait_send()
 
 
     mix_copy.wait()
-    flat = back[...]
-    flat = jnp.concatenate(
-        [flat[:, part].reshape(places * count * HEAD, TILE) for part in range(parts)], axis=1
-    )
-    feats = heads * HEAD
-    rows = [flat[n * feats : (n + 1) * feats].astype(F32).T.astype(BF16) for n in range(seqs)]
+
+    def heads_of(n):
+        tiles = []
+        for part in range(parts):
+            found = []
+            for head in range(heads):
+                place, c = divmod(head * seqs + n, count)
+                found.append(back[place, part, c * HEAD : (c + 1) * HEAD, :].astype(F32))
+            tiles.append(jnp.concatenate(found, axis=0).T)
+        return jnp.concatenate(tiles, axis=0).astype(BF16)
+
+    rows = [heads_of(n) for n in range(seqs)]
     width = mix.shape[1]
     cuts = ready.shape[0]
     piece = width // cuts
@@ -404,6 +446,7 @@
     for cut in range(cuts):
         for step in range(group - 1, 0, -1):
             move(cut, step, partner(group_me, step, group)).wait_send()
+    drain()
 
 
 def shards(
@@ -434,11 +477,10 @@
     vmem = pl.BlockSpec(memory_space=pltpu.VMEM)
     whole = pl.BlockSpec(memory_space=pl.ANY)
     dma = pltpu.SemaphoreType.DMA
-    rows = count * 3 * HEAD + 2 * PAIRS
     out = pl.pallas_call(
         functools.partial(layer_kernel, sizes),
         out_shape=jax.ShapeDtypeStruct((seqs * own, width), BF16),
-        in_specs=[vmem, whole] + [vmem] * 8 + [whole],
+        in_specs=[vmem, whole, vmem, pl.BlockSpec(memory_space=pltpu.SMEM)] + [vmem] * 6 + [whole],
         out_specs=vmem,
         scratch_shapes=[
             pltpu.VMEM((count, inner, TILE), F32),
@@ -451,23 +493,25 @@
             pltpu.VMEM((count, HEAD, TILE), F32),
             pltpu.VMEM((count, HEAD, TILE), F32),
             pltpu.VMEM((count, HEAD, TILE), F32),
-            pltpu.VMEM((places, parts, rows, TILE), BF16),
-            pltpu.VMEM((places, parts, rows, TILE), BF16),
+            pltpu.VMEM((places, count, parts, 3 * HEAD, TILE), BF16),
+            pltpu.VMEM((places, parts, 2 * PAIRS, TILE), BF16),
+            pltpu.VMEM((places, count, parts, 3 * HEAD, TILE), BF16),
+            pltpu.VMEM((places, parts, 2 * PAIRS, TILE), BF16),
             pltpu.VMEM((places, parts, count * HEAD, TILE), BF16),
             pltpu.VMEM((places, parts, count * HEAD, TILE), BF16),
             pltpu.VMEM((pieces, heads * 3 * HEAD, piece), BF16),
-            pltpu.VMEM((heads, 3 * HEAD, seqs * block), F32),
-            pltpu.VMEM((pieces, group, seqs * own, piece), BF16),
+            pltpu.VMEM((heads, 3 * HEAD, block), F32),
+            pltpu.VMEM((seqs, pieces, group, own, piece), BF16),
             pltpu.VMEM((heads * HEAD, width), BF16),
             pltpu.VMEM((cuts, group, seqs * own, width // cuts), BF16),
             pltpu.VMEM((cuts, group, seqs * own, width // cuts), BF16),
             dma((pieces,)),
-            dma((pieces, group)),
-            dma((pieces, group)),
+            dma((seqs, pieces, group)),
+            dma((seqs, pieces, group)),
             dma,
-            dma((places,)),
-            dma((places,)),
-            dma,
+            dma((places, count + 1)),
+            dma((places, count + 1)),
+            dma((2,)),
             dma((places,)),
             dma((places,)),
             dma,
@@ -478,16 +522,16 @@
             collective_id=1, has_side_effects=True, vmem_limit_bytes=56 * 1024 * 1024
         ),
     )(
-        tokens.reshape(seqs * own, width),
+        tokens,
         qkv_weight.reshape(-1, width),
         rate_weight,
-        jnp.broadcast_to(base_rate[:, None], (heads, TILE)),
+        base_rate,
         first_w,
-        first_b[:, None],
-        second_w,
-        second_b[:, None],
-        norm_gain[:, None],
-        norm_shift[:, None],
+        first_b,
+        jnp.swapaxes(second_w, 1, 2),
+        second_b,
+        norm_gain,
+        norm_shift,
         out_weight,
     )
     return out.reshape(tokens.shape)

time: 99.1 us -> 83.2 us (0.84)
  local copies, waits for them, and re-layouts: 11 us -> 1.77 us
  Pallas kernels: 87.4 us -> 81 us
    broadcast_in_dim x5 -> x0, local copies, waits for them, and re-layouts: 6.51 us -> none  [the longest x1 1.32 us: shards(): first_b[:, None]]
    pallas_call x1, Pallas kernels: 87.4 us -> 81 us  [shards(): pl.pallas_call(functools.partial(layer_kernel, sizes), out_shape=jax.Shap...]
    unnamed x2 -> x1, local copies, waits for them, and re-layouts: 4.53 us -> 1.77 us
where the time goes in v4:
time: 83.2 us; the launch traced here: 82.8 us
  Pallas kernels  81 us (97%)
  local copies, waits for them, and re-layouts  1.77 us (2%)
    pallas_call x1, Pallas kernels, shards(): pl.pallas_call(functools.partial(layer_kernel, sizes), out_shape=jax.Shap...  81 us
    unnamed x1, local copies, waits for them, and re-layouts  1.77 us

profile of v4, /device:TPU:24, one launch (start us, length us, event | category | flops | bytes accessed | tf_op | source)
XLA Modules:
  0.0 82.8 jit_solution(4290332320158233184)
XLA Ops:
  0.0 81.0 %shard_map.109 = bf16[64,3072]{1,0:T(8,128)(2,1)} custom-call(bf16[2,32,3072]{2,1,0:T(8,128)(2,1)} %mine.1, bf16[2304,3072]{1,0:T(8,128)(2,1)} %bitcast.3, bf16[12,3072]{1,0:T(8,128)(2,1)} %rate_weight.1, f32[12]{0:T(128)} %base.1, f32[12,64,256]{2,1,0:T(8,128)} %first_w.1, f32[12,256]{1,0:T(8,128)} %first_b.1, f32[12,64,256]{2,1,0:T(8,128)} %bitcast.5, ...), custom_call_target="tpu_custom_call" | custom-call | tf_op jit(solution)/shard_map/pallas_call | solution.py:480
  81.0 1.8 %copy.13 = bf16[2,32,3072]{2,1,0:T(8,128)(2,1)} copy(bf16[2,32,3072]{2,1,0:T(8,128)(2,1)} %bitcast.4) | data formatting | bytes 786432

commit v5 on v4

--- a/solution.py
+++ b/solution.py
@@ -201,9 +201,31 @@
             device_id_type=MESH,
         )
 
+    square = group == 4
+    direct = (2, 1) if square else tuple(range(group - 1, 0, -1))
+
+    def relay(n, cut):
+        held, across = ((1, 2), (2, 1))[cut % 2]
+        source = partner(group_me, held, group)
+        return pltpu.make_async_remote_copy(
+            src_ref=land.at[n, cut, source],
+            dst_ref=land.at[n, cut, source],
+            send_sem=token_send.at[n, cut, 3],
+            recv_sem=token_recv.at[n, cut, source],
+            device_id={"tensor": partner(group_me, across, group)},
+            device_id_type=MESH,
+        )
+
+    def receive(n, cut):
+        for step in direct:
+            peer = partner(group_me, step, group)
+            move(n, cut, step, peer, peer).wait_recv()
+        if square:
+            relay(n, cut).start()
+
     for n in range(seqs):
         for cut in range(pieces):
-            for step in range(group - 1, 0, -1):
+            for step in direct:
                 move(n, cut, step, partner(group_me, step, group), group_me).start()
     for cut in range(pieces):
         fetch(cut).start()
@@ -211,15 +233,20 @@
         load[...] = jnp.zeros_like(load)
     between()
     gates = []
+    order = [(n, cut) for n in range(seqs) for cut in range(pieces)]
+    receive(0, 0)
     for n in range(seqs):
         logit = None
         for cut in range(pieces):
             land[n, cut, group_me] = mine[n, :, span(cut)]
             if n == 0:
                 fetch(cut).wait()
-            for step in range(group - 1, 0, -1):
-                peer = partner(group_me, step, group)
-                move(n, cut, step, peer, peer).wait_recv()
+            at = order.index((n, cut)) + 1
+            if at < len(order):
+                receive(*order[at])
+            if square:
+                peer = partner(group_me, 3, group)
+                move(n, cut, 3, peer, peer).wait_recv()
             tokens = land[n, cut].astype(F32).reshape(block, piece).astype(BF16)
             more = dot(rate_weight[:, span(cut)], tokens, NT)
             logit = more if logit is None else logit + more
@@ -259,8 +286,10 @@
     def drain():
         for n in range(seqs):
             for cut in range(pieces):
-                for step in range(group - 1, 0, -1):
+                for step in direct:
                     move(n, cut, step, partner(group_me, step, group), group_me).wait_send()
+                if square:
+                    relay(n, cut).wait_send()
 
     return drain
 
@@ -420,32 +449,56 @@
     cuts = ready.shape[0]
     piece = width // cuts
 
-    def move(cut, step, peer):
+    def move(cut, row, slot, step):
+        peer = partner(group_me, step, group)
         return pltpu.make_async_remote_copy(
-            src_ref=ready.at[cut, peer],
-            dst_ref=shares.at[cut, step],
-            send_sem=share_send.at[cut, step],
-            recv_sem=share_recv.at[cut, step],
+            src_ref=ready.at[cut, partner(group_me, row, group)],
+            dst_ref=shares.at[cut, slot],
+            send_sem=share_send.at[cut, slot],
+            recv_sem=share_recv.at[cut, slot],
             device_id={"tensor": peer},
             device_id_type=MESH,
         )
+
+    def sends(cut):
+        if group != 4:
+            return [(step, step, step) for step in range(group - 1, 0, -1)], None
+        near, far = ((1, 2), (2, 1))[cut % 2]
+        return [(3, 3, near), (near, near, near)], (far, far, far)
+
+    def pass_on(cut):
+        first, later = sends(cut)
+        if later is None:
+            return
+        move(cut, *first[0]).wait_recv()
+        row = partner(group_me, later[0], group)
+        joint = ready[cut, row].astype(F32) + shares[cut, 3].astype(F32)
+        ready[cut, row] = joint.astype(BF16)
+        move(cut, *later).start()
 
     both = jnp.concatenate(rows, axis=0)
     for cut in range(cuts):
         part = dot(both, mix[:, cut * piece : (cut + 1) * piece])
         part = part.reshape(seqs, group, own_rows, piece)
         ready[cut] = jnp.concatenate([part[n] for n in range(seqs)], axis=1).astype(BF16)
-        for step in range(group - 1, 0, -1):
-            move(cut, step, partner(group_me, step, group)).start()
+        for each in sends(cut)[0]:
+            move(cut, *each).start()
+        if cut >= 2:
+            pass_on(cut - 2)
+    for cut in range(cuts - 2, cuts):
+        pass_on(cut)
     for cut in range(cuts):
         result = ready[cut, group_me].astype(F32)
-        for step in range(group - 1, 0, -1):
-            move(cut, step, partner(group_me, step, group)).wait_recv()
-            result = result + shares[cut, step].astype(F32)
+        first, later = sends(cut)
+        ends = first if later is None else [first[1], later]
+        for each in ends:
+            move(cut, *each).wait_recv()
+            result = result + shares[cut, each[1]].astype(F32)
         out[:, cut * piece : (cut + 1) * piece] = result.astype(BF16)
     for cut in range(cuts):
-        for step in range(group - 1, 0, -1):
-            move(cut, step, partner(group_me, step, group)).wait_send()
+        first, later = sends(cut)
+        for each in first + ([] if later is None else [later]):
+            move(cut, *each).wait_send()
     drain()
 
 

time: 83.2 us -> 89.2 us (1.072)
  Pallas kernels: 81 us -> 87.3 us
    pallas_call x1, Pallas kernels: 81 us -> 87.3 us  [shards(): pl.pallas_call(functools.partial(layer_kernel, sizes), out_shape=jax.Shap...]
where the time goes in v5:
time: 89.2 us; the launch traced here: 89 us
  Pallas kernels  87.3 us (98%)
  local copies, waits for them, and re-layouts  1.77 us (2%)
    pallas_call x1, Pallas kernels, shards(): pl.pallas_call(functools.partial(layer_kernel, sizes), out_shape=jax.Shap...  87.3 us

profile of v5, /device:TPU:24, one launch (start us, length us, event | category | flops | bytes accessed | tf_op | source)
XLA Modules:
  0.0 89.0 jit_solution(11503227499230661866)
XLA Ops:
  0.0 87.3 %shard_map.109 = bf16[64,3072]{1,0:T(8,128)(2,1)} custom-call(bf16[2,32,3072]{2,1,0:T(8,128)(2,1)} %mine.1, bf16[2304,3072]{1,0:T(8,128)(2,1)} %bitcast.3, bf16[12,3072]{1,0:T(8,128)(2,1)} %rate_weight.1, f32[12]{0:T(128)} %base.1, f32[12,64,256]{2,1,0:T(8,128)} %first_w.1, f32[12,256]{1,0:T(8,128)} %first_b.1, f32[12,64,256]{2,1,0:T(8,128)} %bitcast.5, ...), custom_call_target="tpu_custom_call" | custom-call | tf_op jit(solution)/shard_map/pallas_call | solution.py:533
  87.3 1.8 %copy.13 = bf16[2,32,3072]{2,1,0:T(8,128)(2,1)} copy(bf16[2,32,3072]{2,1,0:T(8,128)(2,1)} %bitcast.4) | data formatting | bytes 786432

commit v6 on v5

--- a/solution.py
+++ b/solution.py
@@ -201,31 +201,9 @@
             device_id_type=MESH,
         )
 
-    square = group == 4
-    direct = (2, 1) if square else tuple(range(group - 1, 0, -1))
-
-    def relay(n, cut):
-        held, across = ((1, 2), (2, 1))[cut % 2]
-        source = partner(group_me, held, group)
-        return pltpu.make_async_remote_copy(
-            src_ref=land.at[n, cut, source],
-            dst_ref=land.at[n, cut, source],
-            send_sem=token_send.at[n, cut, 3],
-            recv_sem=token_recv.at[n, cut, source],
-            device_id={"tensor": partner(group_me, across, group)},
-            device_id_type=MESH,
-        )
-
-    def receive(n, cut):
-        for step in direct:
-            peer = partner(group_me, step, group)
-            move(n, cut, step, peer, peer).wait_recv()
-        if square:
-            relay(n, cut).start()
-
     for n in range(seqs):
         for cut in range(pieces):
-            for step in direct:
+            for step in range(group - 1, 0, -1):
                 move(n, cut, step, partner(group_me, step, group), group_me).start()
     for cut in range(pieces):
         fetch(cut).start()
@@ -233,20 +211,15 @@
         load[...] = jnp.zeros_like(load)
     between()
     gates = []
-    order = [(n, cut) for n in range(seqs) for cut in range(pieces)]
-    receive(0, 0)
     for n in range(seqs):
         logit = None
         for cut in range(pieces):
             land[n, cut, group_me] = mine[n, :, span(cut)]
             if n == 0:
                 fetch(cut).wait()
-            at = order.index((n, cut)) + 1
-            if at < len(order):
-                receive(*order[at])
-            if square:
-                peer = partner(group_me, 3, group)
-                move(n, cut, 3, peer, peer).wait_recv()
+            for step in range(group - 1, 0, -1):
+                peer = partner(group_me, step, group)
+                move(n, cut, step, peer, peer).wait_recv()
             tokens = land[n, cut].astype(F32).reshape(block, piece).astype(BF16)
             more = dot(rate_weight[:, span(cut)], tokens, NT)
             logit = more if logit is None else logit + more
@@ -286,10 +259,8 @@
     def drain():
         for n in range(seqs):
             for cut in range(pieces):
-                for step in direct:
+                for step in range(group - 1, 0, -1):
                     move(n, cut, step, partner(group_me, step, group), group_me).wait_send()
-                if square:
-                    relay(n, cut).wait_send()
 
     return drain
 

time: 89.2 us -> 80.8 us (0.906)
  Pallas kernels: 87.3 us -> 78.9 us
    pallas_call x1, Pallas kernels: 87.3 us -> 78.9 us  [shards(): pl.pallas_call(functools.partial(layer_kernel, sizes), out_shape=jax.Shap...]
where the time goes in v6:
time: 80.8 us; the launch traced here: 80.6 us
  Pallas kernels  78.9 us (98%)
  local copies, waits for them, and re-layouts  1.77 us (2%)
    pallas_call x1, Pallas kernels, shards(): pl.pallas_call(functools.partial(layer_kernel, sizes), out_shape=jax.Shap...  78.9 us
    unnamed x1, local copies, waits for them, and re-layouts  1.77 us

profile of v6, /device:TPU:24, one launch (start us, length us, event | category | flops | bytes accessed | tf_op | source)
XLA Modules:
  0.0 80.6 jit_solution(13803326134359640891)
XLA Ops:
  0.0 78.9 %shard_map.109 = bf16[64,3072]{1,0:T(8,128)(2,1)} custom-call(bf16[2,32,3072]{2,1,0:T(8,128)(2,1)} %mine.1, bf16[2304,3072]{1,0:T(8,128)(2,1)} %bitcast.3, bf16[12,3072]{1,0:T(8,128)(2,1)} %rate_weight.1, f32[12]{0:T(128)} %base.1, f32[12,64,256]{2,1,0:T(8,128)} %first_w.1, f32[12,256]{1,0:T(8,128)} %first_b.1, f32[12,64,256]{2,1,0:T(8,128)} %bitcast.5, ...), custom_call_target="tpu_custom_call" | custom-call | tf_op jit(solution)/shard_map/pallas_call | solution.py:504
  78.9 1.8 %copy.13 = bf16[2,32,3072]{2,1,0:T(8,128)(2,1)} copy(bf16[2,32,3072]{2,1,0:T(8,128)(2,1)} %bitcast.4) | data formatting | bytes 786432
